TPU v7x, 256 devices: a whole 4x4x8 slice. The times are simulated.
256 devices in a mesh: dp: 32 (over y, z_lo, core), ctx: 8 (over x, z_hi).
Axes of the slice: x: 4, y: 4, z: 8 (z_hi: 2, z_lo: 4; z = z_hi * 4 + z_lo), core: 2. Of those that a mesh axis runs over, the one named last changes fastest.
Arguments:
- query_in: bfloat16 [32768, 4096], P(('dp', 'ctx')), may hold values from -5 to 5
- key_in: bfloat16 [32768, 4096], P(('dp', 'ctx')), may hold values from -5 to 5
- value_in: bfloat16 [32768, 4096], P(('dp', 'ctx')), may hold values from -5 to 5
- grad_out: bfloat16 [32768, 4096], P(('dp', 'ctx')), may hold values from -5 to 5
- filters: bfloat16 [32768, 4096], P('dp', 'ctx'), may hold values from -2 to 2
Outputs:
- gated_out: bfloat16 [32768, 4096], P(('dp', 'ctx'))
- grad_query: bfloat16 [32768, 4096], P(('dp', 'ctx'))
- grad_key: bfloat16 [32768, 4096], P(('dp', 'ctx'))
- grad_value: bfloat16 [32768, 4096], P(('dp', 'ctx'))
All inputs are finite; a program needn't handle non-finite values.
Results may differ from a plain program's by a relative error of at most 0.0087.
Values may be sent and summed in bfloat16 or wider, within the bound.
No kernel may reach another device: no remote copies, remote signals or barrier semaphores. Data moves between devices by JAX's collectives and lax.ppermute only.
A program may use at most 128 MiB of HBM per device.

v0:
```python
import math

import jax
import jax.numpy as jnp
from jax import lax
from jax.sharding import PartitionSpec as P


def counting(number_of, offset_by):
    return offset_by + jnp.arange(number_of, dtype=jnp.int32)


def angles(period, left_index, right_index, direction):
    phase_idx = left_index[:, None] * right_index[None, :] % period
    angle_rad = direction * 2.0 * math.pi / period * phase_idx.astype(jnp.float32)
    return (jnp.cos(angle_rad), jnp.sin(angle_rad))


def complex_table(period, left_index, right_index, direction):
    cos_part, sin_part = angles(period, left_index, right_index, direction)
    return jnp.stack([jnp.stack([cos_part, -sin_part]), jnp.stack([sin_part, cos_part])]).astype(
        jnp.bfloat16
    )


def rotate_round(data, cos_part, sin_part):
    real_part = data[0]
    imag_part = data[1]
    return jnp.stack(
        [real_part * cos_part - imag_part * sin_part, real_part * sin_part + imag_part * cos_part]
    ).astype(jnp.bfloat16)


def apply_filter(filt_spec, gate_spec, grad_spec):
    conv_spec = jnp.stack(
        [
            filt_spec[0] * gate_spec[0] - filt_spec[1] * gate_spec[1],
            filt_spec[0] * gate_spec[1] + filt_spec[1] * gate_spec[0],
        ]
    )
    corr_spec = jnp.stack(
        [
            filt_spec[0] * grad_spec[0] + filt_spec[1] * grad_spec[1],
            filt_spec[0] * grad_spec[1] - filt_spec[1] * grad_spec[0],
        ]
    )
    return (conv_spec.astype(jnp.bfloat16), corr_spec.astype(jnp.bfloat16))


def body(query_in, key_in, value_in, grad_out, filters):
    gate_in = (key_in.astype(jnp.float32) * value_in.astype(jnp.float32)).astype(jnp.bfloat16)
    grad_conv = (grad_out.astype(jnp.float32) * query_in.astype(jnp.float32)).astype(jnp.bfloat16)
    gate_cols, grad_cols = (
        lax.all_to_all(gate_in, "ctx", split_axis=1, concat_axis=0, tiled=True),
        lax.all_to_all(grad_conv, "ctx", split_axis=1, concat_axis=0, tiled=True),
    )
    row_count, col_width = gate_cols.shape
    block_count = lax.axis_size("dp")
    wave_count = 2 * block_count
    period = wave_count * row_count
    outer_count = max(1, row_count // 128)
    inner_count = row_count // outer_count
    outer_idx = counting(outer_count, 0)
    inner_idx = counting(inner_count, 0)
    fwd_cos, fwd_sin = angles(wave_count, counting(wave_count, 0), counting(block_count, 0), -1.0)
    section_fwd = jnp.stack([fwd_cos, fwd_sin]).astype(jnp.bfloat16)
    bwd_cos, bwd_sin = angles(wave_count, counting(block_count, 0), counting(wave_count, 0), 1.0)
    section_bwd = jnp.stack([bwd_cos, -bwd_sin]).astype(jnp.bfloat16)
    outer_fwd = complex_table(outer_count, outer_idx, outer_idx, -1.0)
    outer_bwd = complex_table(outer_count, outer_idx, outer_idx, 1.0)
    inner_fwd = complex_table(inner_count, inner_idx, inner_idx, -1.0)
    inner_bwd = complex_table(inner_count, inner_idx, inner_idx, 1.0)
    mid_fc, mid_fs = angles(row_count, outer_idx, inner_idx, -1.0)
    mid_bc, mid_bs = angles(row_count, outer_idx, inner_idx, 1.0)
    position = lax.axis_index("dp")
    piece_rows = row_count // block_count
    signal = jnp.concatenate([filters, gate_cols, grad_cols], axis=1)
    blocks = lax.all_to_all(
        signal.reshape(1, row_count, 3 * col_width), "dp", split_axis=1, concat_axis=0, tiled=True
    )
    mid = jnp.einsum("zkp,prc->zkrc", section_fwd, blocks, preferred_element_type=jnp.float32)
    twist_fc, twist_fs = angles(
        period, counting(wave_count, 0), counting(piece_rows, position * piece_rows), -1.0
    )
    part = rotate_round(mid, twist_fc[:, :, None], twist_fs[:, :, None])
    got = lax.all_to_all(part, "dp", split_axis=1, concat_axis=2, tiled=True)
    local_waves = got.shape[1]
    got = got.reshape(2, local_waves, outer_count, inner_count, 3 * col_width)
    middle = jnp.einsum("zyka,ywavc->zwkvc", outer_fwd, got, preferred_element_type=jnp.float32)
    middle = rotate_round(middle, mid_fc[None, :, :, None], mid_fs[None, :, :, None])
    spectrum = jnp.einsum(
        "zyjv,ywkvc->zwkjc", inner_fwd, middle, preferred_element_type=jnp.float32
    )
    conv_spec, corr_spec = apply_filter(
        spectrum[..., :col_width],
        spectrum[..., col_width : 2 * col_width],
        spectrum[..., 2 * col_width :],
    )
    both_spec = jnp.concatenate([conv_spec, corr_spec], axis=4)
    unmixed = jnp.einsum(
        "zyvj,ywkjc->zwkvc", inner_bwd, both_spec, preferred_element_type=jnp.float32
    )
    unmixed = rotate_round(unmixed, mid_bc[None, :, :, None], mid_bs[None, :, :, None])
    back = jnp.einsum(
        "zyak,ywkvc->zwavc", outer_bwd, unmixed, preferred_element_type=jnp.float32
    ).astype(jnp.bfloat16)
    back = back.reshape(2, local_waves, row_count, 2 * col_width)
    recv = lax.all_to_all(back, "dp", split_axis=2, concat_axis=1, tiled=True).astype(jnp.float32)
    twist_bc, twist_bs = angles(
        period, counting(wave_count, 0), counting(piece_rows, position * piece_rows), 1.0
    )
    spun = rotate_round(recv, twist_bc[:, :, None], twist_bs[:, :, None])
    values = jnp.einsum("zpk,zkrc->prc", section_bwd, spun, preferred_element_type=jnp.float32)
    rounded = (values * (1.0 / period)).astype(jnp.bfloat16)
    merged = lax.all_to_all(rounded, "dp", split_axis=0, concat_axis=1, tiled=True).reshape(
        row_count, 2 * col_width
    )
    conv_out = merged[:, :col_width]
    corr_out = merged[:, col_width:]
    conv_tok, corr_tok = (
        lax.all_to_all(conv_out, "ctx", split_axis=0, concat_axis=1, tiled=True),
        lax.all_to_all(corr_out, "ctx", split_axis=0, concat_axis=1, tiled=True),
    )
    conv_wide = conv_tok.astype(jnp.float32)
    corr_wide = corr_tok.astype(jnp.float32)
    gated_out = (query_in.astype(jnp.float32) * conv_wide).astype(jnp.bfloat16)
    grad_query = (grad_out.astype(jnp.float32) * conv_wide).astype(jnp.bfloat16)
    grad_key = (corr_wide * value_in.astype(jnp.float32)).astype(jnp.bfloat16)
    grad_value = (corr_wide * key_in.astype(jnp.float32)).astype(jnp.bfloat16)
    return (gated_out, grad_query, grad_key, grad_value)


def solution(mesh):
    return jax.shard_map(
        body,
        mesh=mesh,
        in_specs=(
            P(("dp", "ctx"), None),
            P(("dp", "ctx"), None),
            P(("dp", "ctx"), None),
            P(("dp", "ctx"), None),
            P("dp", "ctx"),
        ),
        out_specs=(
            P(("dp", "ctx"), None),
            P(("dp", "ctx"), None),
            P(("dp", "ctx"), None),
            P(("dp", "ctx"), None),
        ),
        check_vma=False,
    )
```

profile of v0, /device:TPU:1, one launch (start us, length us, event | category | flops | bytes accessed | tf_op | source)
XLA Modules:
  0.0 1109.0 jit_solution(4254387484054342472)
XLA Ops:
  5.9 11.5 %all-to-all-start = ((bf16[128,8,512]{2,0,1:T(8,128)(2,1)}), bf16[128,8,512]{2,0,1:T(8,128)(2,1)}, u32[]{:S(2)}, u32[]{:S(2)}) async-start(bf16[128,8,512]{2,0,1:T(8,128)(2,1)} %copy.107), calls=%async_computation | async-start | bytes 2097152 | tf_op jit(solution)/shard_map/all_to_all | solution.py:54
  22.6 15.9 %all-to-all-done = bf16[128,8,512]{2,0,1:T(8,128)(2,1)} async-done(((bf16[128,8,512]{2,0,1:T(8,128)(2,1)}), bf16[128,8,512]{2,0,1:T(8,128)(2,1)}, u32[]{:S(2)}, u32[]{:S(2)}) %all-to-all-start) | async-done | bytes 1048608 | tf_op jit(solution)/shard_map/all_to_all | solution.py:54
  38.5 18.0 %all_to_all.109 = bf16[128,8,512]{2,0,1:T(8,128)(2,1)S(1)} all-to-all(bf16[128,8,512]{2,0,1:T(8,128)(2,1)} %copy.109), channel_id=1, replica_groups=mesh['dp'=32,'ctx'=8] {'ctx'}, dimensions={1} | all-to-all | bytes 2097152 | tf_op jit(solution)/shard_map/all_to_all | solution.py:55
  58.1 35.0 %copy.163 = bf16[1,1024,1536]{2,0,1:T(2,128)(2,1)} copy(bf16[1,1024,1536]{2,1,0:T(8,128)(2,1)S(1)} %maximum_bitcast_fusion.6) | data formatting | bytes 6291456 | tf_op jit(solution)/shard_map/reshape | solution.py:79
  93.6 20.3 %reduce = bf16[1024,1536]{1,0:T(8,128)(2,1)S(1)} reduce(bf16[1024,1,1536]{2,1,0:T(2,128)(2,1)} %bitcast.132, bf16[]{:T(256)} %broadcast.856), dimensions={1}, to_apply=%bitcast.128.reduce_sub_computation | reduce | bytes 6291458
  114.0 3.5 reshape.586
  117.5 26.0 %all-to-all-start.2 = ((bf16[32,2,24576]{2,1,0:T(2,128)(2,1)}), bf16[32,2,24576]{2,1,0:T(2,128)(2,1)S(1)}, u32[]{:S(2)}, u32[]{:S(2)}) async-start(bf16[32,2,24576]{2,1,0:T(2,128)(2,1)} %reshape.586), calls=%async_computation.2 | async-start | bytes 6291456 | tf_op jit(solution)/shard_map/all_to_all | solution.py:78
  144.4 70.9 %all-to-all-done.2 = bf16[32,2,24576]{2,1,0:T(2,128)(2,1)S(1)} async-done(((bf16[32,2,24576]{2,1,0:T(2,128)(2,1)}), bf16[32,2,24576]{2,1,0:T(2,128)(2,1)S(1)}, u32[]{:S(2)}, u32[]{:S(2)}) %all-to-all-start.2) | async-done | bytes 3145760 | tf_op jit(solution)/shard_map/all_to_all | solution.py:78
  215.4 12.4 %reshape.587 = bf16[1024,1,1536]{2,1,0:T(2,128)(2,1)} reshape(bf16[32,2,24576]{2,1,0:T(2,128)(2,1)S(1)} %all-to-all-done.2) | data formatting | bytes 6291456
  227.8 5.3 copy.153
  233.1 6.7 fusion.16
  239.8 6.3 subtract_convert_fusion.1
  246.1 4.8 pad_maximum_fusion
  250.9 24.0 %copy.112 = bf16[2,64,32,1536]{3,2,0,1:T(8,128)(2,1)} copy(bf16[2,64,32,1536]{3,1,2,0:T(8,128)(2,1)S(1)} %pad_maximum_fusion) | data formatting | bytes 25165824 | tf_op jit(solution)/shard_map/stack | solution.py:29
  274.9 6.2 all-to-all-start.3
  282.9 272.4 %all-to-all-done.3 = bf16[2,64,32,1536]{3,2,0,1:T(8,128)(2,1)} async-done(((bf16[2,64,32,1536]{3,2,0,1:T(8,128)(2,1)}), bf16[2,64,32,1536]{3,2,0,1:T(8,128)(2,1)}, u32[]{:S(2)}, u32[]{:S(2)}) %all-to-all-start.3) | async-done | bytes 12582944 | tf_op jit(solution)/shard_map/all_to_all | solution.py:86
  555.3 11.0 copy.114
  566.3 17.4 %convolution_bitcast_fusion.1 = f32[2,2,8,128,1536]{4,2,0,3,1:T(8,128)} fusion(bf16[2,2,8,128,1536,1]{4,3,2,1,0,5:T(8,128)(2,1)} %bitcast.129, bf16[1,2,8,8]{3,2,1,0:T(8,128)(2,1)S(1)} %get-tuple-element.47, bf16[1,2,8,8]{3,2,1,0:T(8,128)(2,1)S(1)} %get-tuple-element.46), kind=kOutput, calls=%fused_computation.3 | convolution fusion | flops 201327616 | bytes 37749248 | tf_op jit(solution)/shard_map/zyka,ywavc->zwkvc/dot_general | solution.py:89
  583.6 10.2 subtract_convert_fusion
  595.1 29.1 %convolution_bitcast_fusion = f32[2,2,8,128,1536]{3,4,0,2,1:T(8,128)} fusion(bf16[2,2,8,128,1536,1]{4,2,0,3,1,5:T(8,128)(2,1)S(1)} %maximum_bitcast_fusion, bf16[1,2,128,128]{3,2,1,0:T(8,128)(2,1)S(1)} %get-tuple-element.43, bf16[1,2,128,128]{3,2,1,0:T(8,128)(2,1)S(1)} %get-tuple-element.42), kind=kOutput, calls=%fused_computation.2 | convolution fusion | flops 3221487616 | bytes 37879808 | tf_op jit(solution)/shard_map/zyjv,ywkvc->zwkjc/dot_general | solution.py:91
  624.3 11.6 %subtract_convert_fusion.5 = (bf16[1,2,8,128,512]{3,4,0,2,1:T(8,128)(2,1)S(1)}, bf16[1,2,8,128,512]{3,4,0,2,1:T(8,128)(2,1)S(1)}, bf16[1,2,8,128,512]{3,4,0,2,1:T(8,128)(2,1)}, bf16[1,2,8,128,512]{3,4,0,2,1:T(8,128)(2,1)}) fusion(f32[2,2,8,128,1536]{3,4,0,2,1:T(8,128)} %convolution_bitcast_fusion), kind=kLoop, calls=%fused_computation.36 | loop fusion | flops 16777216 | bytes 33554432 | tf_op jit(solution)/shard_map/convert.28
  635.8 4.7 fusion.14
  640.6 3.6 subtract_convert_fusion.3
  644.2 6.2 maximum_bitcast_fusion.3
  650.4 12.3 %copy.142 = bf16[2,2,8,128,1024,1]{4,2,0,5,3,1:T(8,128)(2,1)} copy(bf16[2,2,8,128,1024,1]{3,4,0,2,1,5:T(8,128)(2,1)} %maximum_bitcast_fusion.3) | data formatting | bytes 16777216 | tf_op jit(solution)/shard_map/stack | solution.py:29
  662.8 10.4 fusion.2
  673.2 11.4 %copy.120 = bf16[2,2,8,128,1024]{4,3,2,1,0:T(8,128)(2,1)} copy(bf16[2,2,8,128,1024]{4,2,0,3,1:T(8,128)(2,1)} %fusion.2) | data formatting | bytes 16777216 | tf_op jit(solution)/shard_map/convert_element_type | solution.py:106
  684.6 16.6 %copy.121 = bf16[2,2,1024,1024]{3,1,0,2:T(2,128)(2,1)} copy(bf16[2,2,1024,1024]{3,2,1,0:T(8,128)(2,1)} %bitcast.131) | data formatting | bytes 16777216 | tf_op jit(solution)/shard_map/reshape | solution.py:107
  701.2 5.8 all-to-all-start.4
  707.0 184.4 %all-to-all-done.4 = bf16[2,2,1024,1024]{3,1,0,2:T(2,128)(2,1)} async-done(((bf16[2,2,1024,1024]{3,1,0,2:T(2,128)(2,1)}), bf16[2,2,1024,1024]{3,1,0,2:T(2,128)(2,1)}, u32[]{:S(2)}, u32[]{:S(2)}) %all-to-all-start.4) | async-done | bytes 8388640 | tf_op jit(solution)/shard_map/all_to_all | solution.py:108
  891.4 9.5 copy.122
  900.9 11.4 %convert_bitcast_fusion = f32[2,32,2,32,1024]{4,3,1,2,0:T(8,128)} fusion(bf16[2,2,32,32,1024]{4,3,2,1,0:T(8,128)(2,1)} %bitcast.130), kind=kLoop, calls=%fused_computation | loop fusion | flops 4194304 | bytes 25165824 | tf_op jit(solution)/shard_map/convert_element_type | solution.py:108
  912.3 9.4 fusion.81
  921.7 9.1 copy.123
  930.9 11.0 slice.86
  941.8 15.4 %copy.124 = f32[1,32,2,32,1024]{4,2,1,3,0:T(2,128)} copy(f32[1,32,2,32,1024]{4,3,1,2,0:T(8,128)} %get-tuple-element.33) | data formatting | bytes 16777216 | tf_op jit(solution)/shard_map/slice | solution.py:28
  957.2 11.0 slice.88
  968.2 7.0 subtract_convert_fusion.2
  978.1 54.9 %all_to_all.110 = bf16[32,32,1024]{2,1,0:T(8,128)(2,1)S(1)} all-to-all(bf16[32,32,1024]{2,1,0:T(8,128)(2,1)S(1)} %copy.125), channel_id=1, replica_groups=mesh['dp'=32,'ctx'=8] {'dp'}, dimensions={0} | all-to-all | bytes 4194304 | tf_op jit(solution)/shard_map/all_to_all | solution.py:115
  1034.2 30.8 %all_to_all.111 = bf16[8,128,512]{2,1,0:T(8,128)(2,1)} all-to-all(bf16[8,128,512]{2,1,0:T(8,128)(2,1)S(1)} %bitcast.138), channel_id=1, replica_groups=mesh['dp'=32,'ctx'=8] {'ctx'}, dimensions={0} | all-to-all | bytes 2097152 | tf_op jit(solution)/shard_map/all_to_all | solution.py:122
  1065.0 4.8 all-to-all-start.6
  1073.2 3.7 fusion.22
  1076.9 2.3 copy.130
  1079.1 2.3 copy.131
  1081.4 14.8 %all-to-all-done.6 = bf16[8,128,512]{2,1,0:T(8,128)(2,1)} async-done(((bf16[8,128,512]{2,1,0:T(8,128)(2,1)}), bf16[8,128,512]{2,1,0:T(8,128)(2,1)}, u32[]{:S(2)}, u32[]{:S(2)}) %all-to-all-start.6) | async-done | bytes 1048608 | tf_op jit(solution)/shard_map/all_to_all | solution.py:121
  1096.2 2.9 convert_bitcast_fusion.2
  1099.1 2.9 copy.126
  1102.0 3.0 fusion.26
  (57 shorter events, 27.4 us)
Async XLA Ops:
  2.3 3.6 copy-start.4
  4.3 13.1 %copy-start.6 = (bf16[128,4096]{0,1:T(8,128)(2,1)}, bf16[128,4096]{0,1:T(8,128)(2,1)S(1)}, u32[]{:S(2)}) copy-start(bf16[128,4096]{0,1:T(8,128)(2,1)S(1)} %copy.106) | copy-start | bytes 3145732
  5.9 32.6 %all-to-all-start = ((bf16[128,8,512]{2,0,1:T(8,128)(2,1)}), bf16[128,8,512]{2,0,1:T(8,128)(2,1)}, u32[]{:S(2)}, u32[]{:S(2)}) async-start(bf16[128,8,512]{2,0,1:T(8,128)(2,1)} %copy.107), calls=%async_computation | async-start | bytes 2097152 | tf_op jit(solution)/shard_map/all_to_all | solution.py:54
  19.0 74.1 %copy-start = (bf16[128,4096]{0,1:T(8,128)(2,1)}, bf16[128,4096]{0,1:T(8,128)(2,1)S(1)}, u32[]{:S(2)}) copy-start(bf16[128,4096]{0,1:T(8,128)(2,1)S(1)} %copy.104) | copy-start | bytes 3145732
  21.0 72.1 %copy-start.2 = (bf16[128,4096]{0,1:T(8,128)(2,1)}, bf16[128,4096]{0,1:T(8,128)(2,1)S(1)}, u32[]{:S(2)}) copy-start(bf16[128,4096]{0,1:T(8,128)(2,1)S(1)} %copy.108) | copy-start | bytes 3145732
  117.5 97.9 %all-to-all-start.2 = ((bf16[32,2,24576]{2,1,0:T(2,128)(2,1)}), bf16[32,2,24576]{2,1,0:T(2,128)(2,1)S(1)}, u32[]{:S(2)}, u32[]{:S(2)}) async-start(bf16[32,2,24576]{2,1,0:T(2,128)(2,1)} %reshape.586), calls=%async_computation.2 | async-start | bytes 6291456 | tf_op jit(solution)/shard_map/all_to_all | solution.py:78
  274.9 280.4 %all-to-all-start.3 = ((bf16[2,64,32,1536]{3,2,0,1:T(8,128)(2,1)}), bf16[2,64,32,1536]{3,2,0,1:T(8,128)(2,1)}, u32[]{:S(2)}, u32[]{:S(2)}) async-start(bf16[2,64,32,1536]{3,2,0,1:T(8,128)(2,1)} %copy.112), calls=%async_computation.3 | async-start | bytes 25165824 | tf_op jit(solution)/shard_map/all_to_all | solution.py:86
  701.2 190.2 %all-to-all-start.4 = ((bf16[2,2,1024,1024]{3,1,0,2:T(2,128)(2,1)}), bf16[2,2,1024,1024]{3,1,0,2:T(2,128)(2,1)}, u32[]{:S(2)}, u32[]{:S(2)}) async-start(bf16[2,2,1024,1024]{3,1,0,2:T(2,128)(2,1)} %copy.121), calls=%async_computation.4 | async-start | bytes 16777216 | tf_op jit(solution)/shard_map/all_to_all | solution.py:108
  957.2 11.0 copy-start.7
  957.2 11.0 copy-start.8
  1033.0 40.1 %copy-start.5 = (bf16[128,4096]{0,1:T(8,128)(2,1)S(1)}, bf16[128,4096]{0,1:T(8,128)(2,1)}, u32[]{:S(2)}) copy-start(bf16[128,4096]{0,1:T(8,128)(2,1)} %copy-done.4) | copy-start | bytes 3145732
  1065.0 31.2 %all-to-all-start.6 = ((bf16[8,128,512]{2,1,0:T(8,128)(2,1)}), bf16[8,128,512]{2,1,0:T(8,128)(2,1)}, u32[]{:S(2)}, u32[]{:S(2)}) async-start(bf16[8,128,512]{2,1,0:T(8,128)(2,1)} %bitcast.58), calls=%async_computation.6 | async-start | bytes 2097152 | tf_op jit(solution)/shard_map/all_to_all | solution.py:121
  1073.2 28.8 %copy-start.1 = (bf16[128,4096]{0,1:T(8,128)(2,1)S(1)}, bf16[128,4096]{0,1:T(8,128)(2,1)}, u32[]{:S(2)}) copy-start(bf16[128,4096]{0,1:T(8,128)(2,1)} %copy-done) | copy-start | bytes 3145732
  1073.2 28.8 %copy-start.3 = (bf16[128,4096]{0,1:T(8,128)(2,1)S(1)}, bf16[128,4096]{0,1:T(8,128)(2,1)}, u32[]{:S(2)}) copy-start(bf16[128,4096]{0,1:T(8,128)(2,1)} %copy-done.2) | copy-start | bytes 3145732
where the time goes:
time: 1120 us; the launch traced here: 1110 us
  waiting for transfers between devices  558 us (50%)
  local copies, waits for them, and re-layouts  223 us (20%)
  blocking collectives  104 us (9%)
  other arithmetic  98.3 us (9%)
  matrix products  70.1 us (6%)
  starting transfers between devices  54.3 us (5%)
    all_to_all x1, waiting for transfers between devices, body(): got = lax.all_to_all(part, 'dp', split_axis=1, concat_axis=2, tiled=True)  272 us
    all_to_all x1, waiting for transfers between devices, body(): lax.all_to_all(back, 'dp', split_axis=2, concat_axis=1, tiled=True)  184 us
    all_to_all x1, waiting for transfers between devices, body(): lax.all_to_all(signal.reshape(1, row_count, 3 * col_width), 'dp', split_a...  70.9 us
    all_to_all x1, blocking collectives, body(): lax.all_to_all(rounded, 'dp', split_axis=0, concat_axis=1, tiled=True)  54.9 us
    another operation x15, other arithmetic  40.1 us
    unnamed x30, local copies, waits for them, and re-layouts  37.1 us
    another operation x2, local copies, waits for them, and re-layouts, rotate_round(): jnp.stack([real_part * cos_part - imag_part * sin_part, real_part * sin_p...  36.4 us
    reshape x1, local copies, waits for them, and re-layouts, body(): signal.reshape(1, row_count, 3 * col_width)  35 us
  transfers between devices with their start and end apart: 5, of which 5 were waited for; matrix products, arithmetic and copies ran while one was open for 2% of the time, Pallas kernels for 0%

commit v1 on v0

v1 whole, which is shorter than its diff:
```python
import functools

import jax
import jax.numpy as jnp
import ml_dtypes
import numpy as np
from jax import lax
from jax.experimental import pallas as pl
from jax.experimental.pallas import tpu as pltpu
from jax.sharding import PartitionSpec as P

LANES = 128


def tables(length):
    rows = length // LANES
    period = 2 * length
    freq = np.arange(rows) + 0.5
    outer = 2.0 * np.pi / (2 * rows) * np.outer(freq, np.arange(rows))
    inner = 2.0 * np.pi / LANES * (np.outer(np.arange(LANES), np.arange(LANES)) % LANES)
    spin = 2.0 * np.pi / period * np.outer(freq, np.arange(LANES))
    cos, sin = np.cos(inner), np.sin(inner)
    kind = ml_dtypes.bfloat16
    outer_fwd = np.concatenate([np.cos(outer), -np.sin(outer)], axis=0).astype(kind)
    inner_fwd = np.block([[cos, -sin], [sin, cos]]).astype(kind)
    inner_bwd = np.block([[cos, sin], [-sin, cos]]).astype(kind)
    scale = np.float32(2.0 / period)
    outer_bwd = np.concatenate([np.cos(outer).T, -np.sin(outer).T], axis=1).astype(kind)
    outer_bwd = (outer_bwd.astype(np.float32) * scale).astype(kind)
    spin_cos = np.cos(spin).astype(np.float32)
    spin_sin = np.sin(spin).astype(np.float32)
    return outer_fwd, inner_fwd, inner_bwd, outer_bwd, spin_cos, spin_sin


def pack_kernel(query, key, value, grad, filt, out, lined, spread):
    group = pl.program_id(0)
    width = query.shape[1]
    owners = out.shape[0]
    per_owner = out.shape[2]
    pairs = (key, value), (grad, query)
    for slot, (left, right) in enumerate(pairs):
        prod = left[...].astype(jnp.float32) * right[...].astype(jnp.float32)
        lined[...] = prod.T
        for j in range(2):
            spread[slot, pl.ds(2 * group + j, owners, stride=per_owner), :] = lined[
                pl.ds(j, owners, stride=2), :
            ]
    spread[2, pl.ds(group, width, stride=per_owner // 2), :] = filt[...].astype(jnp.float32).T

    @pl.when(group == pl.num_programs(0) - 1)
    def _():
        for slot in range(3):
            out[:, slot] = (
                spread[slot].reshape(owners, per_owner, LANES).astype(jnp.bfloat16)
            )


def pack(query, key, value, grad, filt, owners):
    tokens, channels = query.shape
    groups = channels // filt.shape[1]
    width = filt.shape[1]
    per_owner = channels // owners
    column = pl.BlockSpec((tokens, width), lambda i: (0, i))
    return pl.pallas_call(
        pack_kernel,
        grid=(groups,),
        in_specs=[column, column, column, column, pl.BlockSpec((tokens, width), lambda i: (i, 0))],
        out_specs=pl.BlockSpec((owners, 3, per_owner, LANES), lambda i: (0, 0, 0, 0)),
        out_shape=jax.ShapeDtypeStruct((owners, 3, per_owner, LANES), jnp.bfloat16),
        scratch_shapes=[
            pltpu.VMEM((width, LANES), jnp.float32),
            pltpu.VMEM((3, owners * per_owner, LANES), jnp.float32),
        ],
        compiler_params=pltpu.CompilerParams(vmem_limit_bytes=48 << 20),
    )(query, key, value, grad, filt)


def mix_kernel(blocks, outer_fwd, inner_fwd, inner_bwd, outer_bwd, cos, sin, out, wide, done):
    blocks_p, groups, _, per_owner, _ = blocks.shape
    rows = blocks_p * groups
    for slot in range(2):
        wide[slot] = (
            blocks[:, :, slot].astype(jnp.float32).reshape(rows * per_owner, LANES)
        )

    def dot(left, right):
        return jnp.dot(left, right, preferred_element_type=jnp.float32)

    def forward(pair):
        mid = dot(outer_fwd[...], jnp.concatenate(pair, axis=1).astype(jnp.bfloat16))
        result = []
        for j in range(2):
            real = mid[:rows, j * LANES : (j + 1) * LANES]
            imag = mid[rows:, j * LANES : (j + 1) * LANES]
            spun = jnp.concatenate(
                [real * cos[...] + imag * sin[...], imag * cos[...] - real * sin[...]], axis=1
            ).astype(jnp.bfloat16)
            both = dot(spun, inner_fwd[...])
            result.append((both[:, :LANES], both[:, LANES:]))
        return result

    def backward(pair):
        spun = []
        for real, imag in pair:
            spec = jnp.concatenate([real, imag], axis=1).astype(jnp.bfloat16)
            both = dot(spec, inner_bwd[...])
            real, imag = both[:, :LANES], both[:, LANES:]
            spun.append(
                jnp.concatenate(
                    [real * cos[...] - imag * sin[...], real * sin[...] + imag * cos[...]], axis=0
                ).astype(jnp.bfloat16)
            )
        return dot(outer_bwd[...], jnp.concatenate(spun, axis=1))

    def step(group, carry):
        filt = blocks[:, group, 2].astype(jnp.float32)
        half = per_owner // 2
        filt_spec = forward([filt[:, j * half : (j + 1) * half].reshape(rows, LANES) for j in range(2)])
        for slot in range(2):
            spec = forward(
                [wide[slot, pl.ds(2 * group + j, rows, stride=per_owner), :] for j in range(2)]
            )
            mixed = []
            for (fr, fi), (gr, gi) in zip(filt_spec, spec):
                if slot == 0:
                    mixed.append((fr * gr - fi * gi, fr * gi + fi * gr))
                else:
                    mixed.append((fr * gr + fi * gi, fr * gi - fi * gr))
            result = backward(mixed)
            for j in range(2):
                done[slot, pl.ds(2 * group + j, rows, stride=per_owner), :] = result[
                    :, j * LANES : (j + 1) * LANES
                ]
        return carry

    lax.fori_loop(0, groups, step, 0)
    for slot in range(2):
        out[:, slot] = done[slot].reshape(rows, per_owner, LANES).astype(jnp.bfloat16)


def mix(blocks, groups):
    rows, _, per_owner, _ = blocks.shape
    consts = [jnp.asarray(t) for t in tables(rows * LANES)]
    return pl.pallas_call(
        mix_kernel,
        out_shape=jax.ShapeDtypeStruct((rows, 2, per_owner, LANES), jnp.bfloat16),
        scratch_shapes=[
            pltpu.VMEM((2, rows * per_owner, LANES), jnp.float32),
            pltpu.VMEM((2, rows * per_owner, LANES), jnp.float32),
        ],
        compiler_params=pltpu.CompilerParams(vmem_limit_bytes=56 << 20),
    )(blocks.reshape(rows // groups, groups, 3, per_owner, LANES), *consts)


def gate_kernel(sums, query, key, value, grad, gated, grad_query, grad_key, grad_value, wide, lined):
    group = pl.program_id(0)
    owners, _, per_owner, _ = sums.shape

    @pl.when(group == 0)
    def _():
        for slot in range(2):
            wide[slot] = sums[:, slot].astype(jnp.float32).reshape(owners * per_owner, LANES)

    uses = ((query, gated), (grad, grad_query)), ((value, grad_key), (key, grad_value))
    for slot in range(2):
        for j in range(2):
            lined[pl.ds(j, owners, stride=2), :] = wide[
                slot, pl.ds(2 * group + j, owners, stride=per_owner), :
            ]
        tokens = lined[...].T
        for source, target in uses[slot]:
            target[...] = (source[...].astype(jnp.float32) * tokens).astype(jnp.bfloat16)


def gate(sums, query, key, value, grad, width):
    tokens, channels = query.shape
    owners, _, per_owner, _ = sums.shape
    groups = channels // width
    column = pl.BlockSpec((tokens, width), lambda i: (0, i))
    return pl.pallas_call(
        gate_kernel,
        grid=(groups,),
        in_specs=[pl.BlockSpec(sums.shape, lambda i: (0, 0, 0, 0))] + [column] * 4,
        out_specs=[column] * 4,
        out_shape=[jax.ShapeDtypeStruct((tokens, channels), jnp.bfloat16)] * 4,
        scratch_shapes=[
            pltpu.VMEM((2, owners * per_owner, LANES), jnp.float32),
            pltpu.VMEM((width, LANES), jnp.float32),
        ],
        compiler_params=pltpu.CompilerParams(vmem_limit_bytes=48 << 20),
    )(sums, query, key, value, grad)


def body(query_in, key_in, value_in, grad_out, filters):
    axes = ("dp", "ctx")
    groups = lax.axis_size("ctx")
    owners = lax.axis_size("dp") * groups
    packed = pack(query_in, key_in, value_in, grad_out, filters, owners)
    blocks = lax.all_to_all(packed, axes, split_axis=0, concat_axis=0, tiled=True)
    mixed = mix(blocks, groups)
    sums = lax.all_to_all(mixed, axes, split_axis=0, concat_axis=0, tiled=True)
    return tuple(gate(sums, query_in, key_in, value_in, grad_out, filters.shape[1]))


def solution(mesh):
    tokens = P(("dp", "ctx"), None)
    return jax.shard_map(
        body,
        mesh=mesh,
        in_specs=(tokens, tokens, tokens, tokens, P("dp", "ctx")),
        out_specs=(tokens, tokens, tokens, tokens),
        check_vma=False,
    )
```

time: 1120 us -> 186 us (0.17)
  waiting for transfers between devices: 558 us -> 0 us
  local copies, waits for them, and re-layouts: 223 us -> 6.13 us
  other arithmetic: 98.3 us -> 0 us
  matrix products: 70.1 us -> 0 us
  starting transfers between devices: 54.3 us -> 0 us
  blocking collectives: 104 us -> 151 us
  Pallas kernels: 0 us -> 27.9 us
    all_to_all x5 -> x0, waiting for transfers between devices: 558 us -> none  [the longest x1 272 us: body(): got = lax.all_to_all(part, 'dp', split_axis=1, concat_axis=2, tiled=True)]
    dot_general x6 -> x0, matrix products: 70.1 us -> none  [the longest x1 29.1 us: body(): jnp.einsum('zyjv,ywkvc->zwkjc', inner_fwd, middle, preferred_element_type...]
    slice x6 -> x0, local copies, waits for them, and re-layouts: 57 us -> none  [the longest x3 29.5 us: rotate_round(): real_part = data[0]]
    all_to_all x5 -> x0, starting transfers between devices: 54.3 us -> none  [the longest x1 26 us: body(): lax.all_to_all(signal.reshape(1, row_count, 3 * col_width), 'dp', split_a...]
    another operation x22 -> x0, other arithmetic: 52.4 us -> none
    reshape x2 -> x0, local copies, waits for them, and re-layouts: 51.6 us -> none  [the longest x1 35 us: body(): signal.reshape(1, row_count, 3 * col_width)]
    all_to_all x3 -> x2, blocking collectives: 104 us -> 151 us  [the longest x1 91.1 us: body(): lax.all_to_all(packed, axes, split_axis=0, concat_axis=0, tiled=True)]
    another operation x2 -> x0, local copies, waits for them, and re-layouts: 36.4 us -> none  [rotate_round(): jnp.stack([real_part * cos_part - imag_part * sin_part, real_part * sin_p...]
  transfers between devices with their start and end apart: 5 -> 0, of which waited for: 5 -> 0; matrix products, arithmetic and copies ran while one was open for 2% -> 0% of each run, Pallas kernels for 0% -> 0%
where the time goes in v1:
time: 186 us
  blocking collectives  151 us (81%)
  Pallas kernels  27.9 us (15%)
  local copies, waits for them, and re-layouts  6.13 us (3%)
    all_to_all x1, blocking collectives, body(): lax.all_to_all(packed, axes, split_axis=0, concat_axis=0, tiled=True)  91.1 us
    all_to_all x1, blocking collectives, body(): sums = lax.all_to_all(mixed, axes, split_axis=0, concat_axis=0, tiled=True)  60 us
    pallas_call x1, Pallas kernels, mix(): pl.pallas_call(mix_kernel, out_shape=jax.ShapeDtypeStruct((rows, 2, per_o...  15.7 us
    pallas_call x1, Pallas kernels, gate(): pl.pallas_call(gate_kernel, grid=(groups,), in_specs=[pl.BlockSpec(sums.s...  6.81 us
    unnamed x18, local copies, waits for them, and re-layouts  6.13 us
    pallas_call x1, Pallas kernels, pack(): pl.pallas_call(pack_kernel, grid=(groups,), in_specs=[column, column, col...  5.31 us

profile of v1, /device:TPU:1, one launch (start us, length us, event | category | flops | bytes accessed | tf_op | source)
XLA Modules:
  0.0 185.7 jit_solution(14492229461287874756)
XLA Ops:
  0.6 0.0 copy-start
  0.6 1.2 copy-done
  1.9 0.0 copy-start.2
  1.9 1.2 copy-done.2
  3.1 0.0 copy-start.4
  3.1 1.2 copy-done.4
  4.3 0.0 copy-start.6
  4.3 1.2 copy-done.6
  5.5 0.0 copy-start.8
  5.5 1.2 copy-done.8
  6.8 5.3 %shard_map.138 = bf16[256,3,16,128]{3,2,1,0:T(8,128)(2,1)} custom-call(bf16[128,4096]{1,0:T(8,128)(2,1)S(1)} %copy-done, bf16[128,4096]{1,0:T(8,128)(2,1)S(1)} %copy-done.2, bf16[128,4096]{1,0:T(8,128)(2,1)S(1)} %copy-done.4, bf16[128,4096]{1,0:T(8,128)(2,1)S(1)} %copy-done.6, bf16[1024,512]{1,0:T(8,128)(2,1)S(1)} %copy-done.8), custom_call_target="tpu_custom_call" | custom-call | tf_op jit(solution)/shard_map/pallas_call | solution.py:64
  12.1 91.1 %all_to_all.10 = bf16[256,3,16,128]{3,2,1,0:T(8,128)(2,1)} all-to-all(bf16[256,3,16,128]{3,2,1,0:T(8,128)(2,1)} %shard_map.138), channel_id=1, replica_groups=mesh['dp'=32,'ctx'=8] {'dp','ctx'}, dimensions={0} | all-to-all | bytes 6291456 | tf_op jit(solution)/shard_map/all_to_all | solution.py:199
  103.1 15.7 %shard_map.139 = bf16[256,2,16,128]{3,2,1,0:T(8,128)(2,1)} custom-call(bf16[32,8,3,16,128]{4,3,2,1,0:T(8,128)(2,1)} %bitcast.1, bf16[512,256]{1,0:T(8,128)(2,1)} %constant.12.clone.outer_fwd, bf16[256,256]{1,0:T(8,128)(2,1)} %constant.13.clone.inner_fwd, bf16[256,256]{1,0:T(8,128)(2,1)} %constant.14.clone.inner_bwd, ...), custom_call_target="tpu_custom_call" | custom-call | tf_op jit(solution)/shard_map/pallas_call | solution.py:144
  118.9 0.0 copy-start.1
  118.9 0.0 copy-start.3
  118.9 0.0 copy-start.5
  118.9 0.0 copy-start.7
  118.9 60.0 %all_to_all.11.sums = bf16[256,2,16,128]{3,2,1,0:T(8,128)(2,1)} all-to-all(bf16[256,2,16,128]{3,2,1,0:T(8,128)(2,1)} %shard_map.139), channel_id=1, replica_groups=mesh['dp'=32,'ctx'=8] {'dp','ctx'}, dimensions={0} | all-to-all | bytes 4194304 | tf_op jit(solution)/shard_map/all_to_all | solution.py:201
  178.9 0.0 copy-done.1
  178.9 0.0 copy-done.3
  178.9 0.0 copy-done.5
  178.9 0.0 copy-done.7
  178.9 6.8 %shard_map.140 = (bf16[128,4096]{1,0:T(8,128)(2,1)}, bf16[128,4096]{1,0:T(8,128)(2,1)}, bf16[128,4096]{1,0:T(8,128)(2,1)}, bf16[128,4096]{1,0:T(8,128)(2,1)}) custom-call(bf16[256,2,16,128]{3,2,1,0:T(8,128)(2,1)} %all_to_all.11.sums, bf16[128,4096]{1,0:T(8,128)(2,1)S(1)} %copy-done.1, bf16[128,4096]{1,0:T(8,128)(2,1)S(1)} %copy-done.3, ...), custom_call_target="tpu_custom_call" | custom-call | tf_op jit(solution)/shard_map/pallas_call | solution.py:180
Async XLA Ops:
  0.6 1.2 copy-start
  1.9 1.2 copy-start.2
  3.1 1.2 copy-start.4
  4.3 1.2 copy-start.6
  5.5 1.2 copy-start.8
  118.9 60.0 %copy-start.1 = (bf16[128,4096]{1,0:T(8,128)(2,1)S(1)}, bf16[128,4096]{1,0:T(8,128)(2,1)}, u32[]{:S(2)}) copy-start(bf16[128,4096]{1,0:T(8,128)(2,1)} %query.3) | copy-start | bytes 3145732
  118.9 60.0 %copy-start.3 = (bf16[128,4096]{1,0:T(8,128)(2,1)S(1)}, bf16[128,4096]{1,0:T(8,128)(2,1)}, u32[]{:S(2)}) copy-start(bf16[128,4096]{1,0:T(8,128)(2,1)} %key.3) | copy-start | bytes 3145732
  118.9 60.0 %copy-start.5 = (bf16[128,4096]{1,0:T(8,128)(2,1)S(1)}, bf16[128,4096]{1,0:T(8,128)(2,1)}, u32[]{:S(2)}) copy-start(bf16[128,4096]{1,0:T(8,128)(2,1)} %value.3) | copy-start | bytes 3145732
  118.9 60.0 %copy-start.7 = (bf16[128,4096]{1,0:T(8,128)(2,1)S(1)}, bf16[128,4096]{1,0:T(8,128)(2,1)}, u32[]{:S(2)}) copy-start(bf16[128,4096]{1,0:T(8,128)(2,1)} %grad.3) | copy-start | bytes 3145732

commit v2 on v1

v2 whole, which is shorter than its diff:
```python
import jax
import jax.numpy as jnp
import ml_dtypes
import numpy as np
from jax import lax
from jax.experimental import pallas as pl
from jax.experimental.pallas import tpu as pltpu
from jax.sharding import PartitionSpec as P

LANES = 128


def tables(length):
    rows = length // LANES
    period = 2 * length
    freq = np.arange(rows) + 0.5
    outer = 2.0 * np.pi / (2 * rows) * np.outer(freq, np.arange(rows))
    inner = 2.0 * np.pi / LANES * (np.outer(np.arange(LANES), np.arange(LANES)) % LANES)
    spin = 2.0 * np.pi / period * np.outer(freq, np.arange(LANES))
    cos, sin = np.cos(inner), np.sin(inner)
    kind = ml_dtypes.bfloat16
    outer_fwd = np.concatenate([np.cos(outer), -np.sin(outer)], axis=0).astype(kind)
    inner_fwd = np.block([[cos, -sin], [sin, cos]]).astype(kind)
    inner_bwd = np.block([[cos, sin], [-sin, cos]]).astype(kind)
    scale = np.float32(2.0 / period)
    outer_bwd = np.concatenate([np.cos(outer).T, -np.sin(outer).T], axis=1).astype(kind)
    outer_bwd = (outer_bwd.astype(np.float32) * scale).astype(kind)
    spin_cos = np.cos(spin).astype(np.float32)
    spin_sin = np.sin(spin).astype(np.float32)
    return outer_fwd, inner_fwd, inner_bwd, outer_bwd, spin_cos, spin_sin


def pack_kernel(query, key, value, grad, filt, out, raw, raw_filt, spread, ready, sems, out_sems):
    owners, _, per_owner, _ = out.shape
    half = per_owner // 2
    load_filt = pltpu.make_async_copy(filt, raw_filt, sems.at[4])
    load_filt.start()
    loads = []
    for i, source in enumerate((key, value, grad, query)):
        loads.append(pltpu.make_async_copy(source, raw.at[i], sems.at[i]))
        loads[-1].start()
    stores = []

    def send(slot, first, count):
        some = slice(first, first + count)
        lines = spread[slot, first * per_owner : (first + count) * per_owner]
        ready[slot, some] = lines.reshape(count, per_owner, LANES).astype(jnp.bfloat16)
        stores.append(
            pltpu.make_async_copy(
                ready.at[slot, some], out.at[some, slot], out_sems.at[len(stores)]
            )
        )
        stores[-1].start()

    load_filt.wait()
    for j in range(2):
        for a in range(half):
            lines = raw_filt[a * LANES : (a + 1) * LANES, j * owners : (j + 1) * owners]
            spread[2, pl.ds(j * half + a, owners, stride=per_owner), :] = lines.astype(jnp.float32).T
    send(2, 0, owners)
    for slot in range(2):
        loads[2 * slot].wait()
        loads[2 * slot + 1].wait()
        for i in range(per_owner):
            columns = slice(i * owners, (i + 1) * owners)
            prod = raw[2 * slot, :, columns].astype(jnp.float32) * raw[
                2 * slot + 1, :, columns
            ].astype(jnp.float32)
            spread[slot, pl.ds(i, owners, stride=per_owner), :] = prod.T
        if slot == 0:
            send(slot, 0, owners)
        else:
            for part in range(4):
                send(slot, part * (owners // 4), owners // 4)
    for store in stores:
        store.wait()


def pack(query, key, value, grad, filt, owners):
    tokens, channels = query.shape
    per_owner = channels // owners
    return pl.pallas_call(
        pack_kernel,
        in_specs=[pl.BlockSpec(memory_space=pltpu.HBM)] * 5,
        out_specs=pl.BlockSpec(memory_space=pltpu.HBM),
        out_shape=jax.ShapeDtypeStruct((owners, 3, per_owner, LANES), jnp.bfloat16),
        scratch_shapes=[
            pltpu.VMEM((4, tokens, channels), jnp.bfloat16),
            pltpu.VMEM(filt.shape, jnp.bfloat16),
            pltpu.VMEM((3, owners * per_owner, LANES), jnp.float32),
            pltpu.VMEM((3, owners, per_owner, LANES), jnp.bfloat16),
            pltpu.SemaphoreType.DMA((5,)),
            pltpu.SemaphoreType.DMA((6,)),
        ],
        compiler_params=pltpu.CompilerParams(vmem_limit_bytes=60 << 20),
    )(query, key, value, grad, filt)


def mix_kernel(blocks, outer_fwd, inner_fwd, inner_bwd, outer_bwd, cos, sin, out, wide, done):
    blocks_p, groups, _, per_owner, _ = blocks.shape
    rows = blocks_p * groups
    half = per_owner // 2
    for slot in range(2):
        wide[slot] = (
            blocks[:, :, slot].astype(jnp.float32).reshape(rows * per_owner, LANES)
        )

    def dot(left, right):
        return jnp.dot(left, right, preferred_element_type=jnp.float32)

    def step(group, carry):
        filt = blocks[:, group, 2].astype(jnp.float32)
        lines = [filt[:, j * half : (j + 1) * half].reshape(rows, LANES) for j in range(2)]
        for slot in range(2):
            for j in range(2):
                lines.append(wide[slot, pl.ds(2 * group + j, rows, stride=per_owner), :])
        mid = dot(outer_fwd[...], jnp.concatenate(lines, axis=1).astype(jnp.bfloat16))
        spun = []
        for i in range(6):
            real = mid[:rows, i * LANES : (i + 1) * LANES]
            imag = mid[rows:, i * LANES : (i + 1) * LANES]
            spun.append(jnp.concatenate(
                [real * cos[...] + imag * sin[...], imag * cos[...] - real * sin[...]], axis=1
            ).astype(jnp.bfloat16))
        both = dot(jnp.concatenate(spun, axis=0), inner_fwd[...])
        spec = [
            (both[i * rows : (i + 1) * rows, :LANES], both[i * rows : (i + 1) * rows, LANES:])
            for i in range(6)
        ]
        mixed = []
        for slot in range(2):
            for j in range(2):
                (fr, fi), (gr, gi) = spec[j], spec[2 + 2 * slot + j]
                if slot == 0:
                    real, imag = fr * gr - fi * gi, fr * gi + fi * gr
                else:
                    real, imag = fr * gr + fi * gi, fr * gi - fi * gr
                mixed.append(jnp.concatenate([real, imag], axis=1).astype(jnp.bfloat16))
        both = dot(jnp.concatenate(mixed, axis=0), inner_bwd[...])
        spun = []
        for i in range(4):
            real = both[i * rows : (i + 1) * rows, :LANES]
            imag = both[i * rows : (i + 1) * rows, LANES:]
            spun.append(jnp.concatenate(
                [real * cos[...] - imag * sin[...], real * sin[...] + imag * cos[...]], axis=0
            ).astype(jnp.bfloat16))
        result = dot(outer_bwd[...], jnp.concatenate(spun, axis=1))
        for slot in range(2):
            for j in range(2):
                i = 2 * slot + j
                done[slot, pl.ds(2 * group + j, rows, stride=per_owner), :] = result[
                    :, i * LANES : (i + 1) * LANES
                ]
        return carry

    lax.fori_loop(0, groups, step, 0, unroll=True)
    for slot in range(2):
        out[:, slot] = done[slot].reshape(rows, per_owner, LANES).astype(jnp.bfloat16)


def mix(blocks, groups):
    rows, _, per_owner, _ = blocks.shape
    consts = [jnp.asarray(t) for t in tables(rows * LANES)]
    return pl.pallas_call(
        mix_kernel,
        out_shape=jax.ShapeDtypeStruct((rows, 2, per_owner, LANES), jnp.bfloat16),
        scratch_shapes=[
            pltpu.VMEM((2, rows * per_owner, LANES), jnp.float32),
            pltpu.VMEM((2, rows * per_owner, LANES), jnp.float32),
        ],
        compiler_params=pltpu.CompilerParams(vmem_limit_bytes=24 << 20),
    )(blocks.reshape(rows // groups, groups, 3, per_owner, LANES), *consts)


def gate_kernel(sums, query, key, value, grad, gated, grad_query, grad_key, grad_value, wide, ready, sems):
    owners, _, per_owner, _ = sums.shape
    channels = query.shape[1]
    width = 2 * owners
    uses = ((query, gated), (grad, grad_query)), ((value, grad_key), (key, grad_value))
    stores = []
    for slot in range(2):
        wide[slot] = sums[:, slot].astype(jnp.float32).reshape(owners * per_owner, LANES)
        for group in range(channels // width):
            for j in range(2):
                i = 2 * group + j
                columns = slice(i * owners, (i + 1) * owners)
                tokens = wide[slot, pl.ds(i, owners, stride=per_owner), :].T
                for k, (source, _) in enumerate(uses[slot]):
                    ready[2 * slot + k, :, columns] = (
                        source[:, columns].astype(jnp.float32) * tokens
                    ).astype(jnp.bfloat16)
            columns = pl.ds(group * width, width)
            for k, (_, target) in enumerate(uses[slot]):
                stores.append(
                    pltpu.make_async_copy(
                        ready.at[2 * slot + k, :, columns],
                        target.at[:, columns],
                        sems.at[len(stores)],
                    )
                )
                stores[-1].start()
    for store in stores:
        store.wait()


def gate(sums, query, key, value, grad, width):
    tokens, channels = query.shape
    owners, _, per_owner, _ = sums.shape
    whole = pl.BlockSpec(memory_space=pltpu.VMEM)
    return pl.pallas_call(
        gate_kernel,
        in_specs=[whole] * 5,
        out_specs=[pl.BlockSpec(memory_space=pltpu.HBM)] * 4,
        out_shape=[jax.ShapeDtypeStruct((tokens, channels), jnp.bfloat16)] * 4,
        scratch_shapes=[
            pltpu.VMEM((2, owners * per_owner, LANES), jnp.float32),
            pltpu.VMEM((4, tokens, channels), jnp.bfloat16),
            pltpu.SemaphoreType.DMA((4 * channels // width,)),
        ],
        compiler_params=pltpu.CompilerParams(vmem_limit_bytes=24 << 20),
    )(sums, query, key, value, grad)


def body(query_in, key_in, value_in, grad_out, filters):
    axes = ("dp", "ctx")
    groups = lax.axis_size("ctx")
    owners = lax.axis_size("dp") * groups
    packed = pack(query_in, key_in, value_in, grad_out, filters, owners)
    blocks = lax.all_to_all(packed, axes, split_axis=0, concat_axis=0, tiled=True)
    mixed = mix(blocks, groups)
    sums = lax.all_to_all(mixed, axes, split_axis=0, concat_axis=0, tiled=True)
    return tuple(gate(sums, query_in, key_in, value_in, grad_out, filters.shape[1]))


def solution(mesh):
    tokens = P(("dp", "ctx"), None)
    return jax.shard_map(
        body,
        mesh=mesh,
        in_specs=(tokens, tokens, tokens, tokens, P("dp", "ctx")),
        out_specs=(tokens, tokens, tokens, tokens),
        check_vma=False,
    )
```

time: 186 us -> 170 us (0.914)
  Pallas kernels: 27.9 us -> 18.7 us
  local copies, waits for them, and re-layouts: 6.13 us -> 0.07 us
    pallas_call x1, Pallas kernels: 15.7 us -> 9.42 us  [mix(): pl.pallas_call(mix_kernel, out_shape=jax.ShapeDtypeStruct((rows, 2, per_o...]
    unnamed x18 -> x20, local copies, waits for them, and re-layouts: 6.13 us -> 0.07 us
    pallas_call x2, Pallas kernels: 12.1 us -> 9.28 us  [the longest x1 5.79 us: pack(): pl.pallas_call(pack_kernel, in_specs=[pl.BlockSpec(memory_space=pltpu.HBM...]
where the time goes in v2:
time: 170 us
  blocking collectives  150 us (88%)
  Pallas kernels  18.7 us (11%)
    all_to_all x1, blocking collectives, body(): lax.all_to_all(packed, axes, split_axis=0, concat_axis=0, tiled=True)  91 us
    all_to_all x1, blocking collectives, body(): sums = lax.all_to_all(mixed, axes, split_axis=0, concat_axis=0, tiled=True)  59.1 us
    pallas_call x1, Pallas kernels, mix(): pl.pallas_call(mix_kernel, out_shape=jax.ShapeDtypeStruct((rows, 2, per_o...  9.42 us
    pallas_call x1, Pallas kernels, pack(): pl.pallas_call(pack_kernel, in_specs=[pl.BlockSpec(memory_space=pltpu.HBM...  5.79 us
    pallas_call x1, Pallas kernels, gate(): pl.pallas_call(gate_kernel, in_specs=[whole] * 5, out_specs=[pl.BlockSpec...  3.49 us

profile of v2, /device:TPU:1, one launch (start us, length us, event | category | flops | bytes accessed | tf_op | source)
XLA Modules:
  0.0 169.8 jit_solution(5410131124410499679)
XLA Ops:
  0.6 5.8 %shard_map.138 = bf16[256,3,16,128]{3,2,1,0:T(8,128)(2,1)} custom-call(bf16[128,4096]{1,0:T(8,128)(2,1)} %query.3, bf16[128,4096]{1,0:T(8,128)(2,1)} %key.3, bf16[128,4096]{1,0:T(8,128)(2,1)} %value.3, bf16[128,4096]{1,0:T(8,128)(2,1)} %grad.3, bf16[1024,512]{1,0:T(8,128)(2,1)} %filt.1), custom_call_target="tpu_custom_call" | custom-call | tf_op jit(solution)/shard_map/pallas_call | solution.py:82
  6.4 0.0 copy-start.4
  6.4 0.0 copy-start.5
  6.5 0.0 copy-start.6
  6.5 0.0 copy-start.7
  6.5 0.0 copy-start.8
  6.5 0.0 copy-start.9
  6.5 91.0 %all_to_all.10 = bf16[256,3,16,128]{3,2,1,0:T(8,128)(2,1)S(1)} all-to-all(bf16[256,3,16,128]{3,2,1,0:T(8,128)(2,1)} %shard_map.138), channel_id=1, replica_groups=mesh['dp'=32,'ctx'=8] {'dp','ctx'}, dimensions={0} | all-to-all | bytes 6291456 | tf_op jit(solution)/shard_map/all_to_all | solution.py:229
  97.5 0.0 copy-done.4
  97.5 0.0 copy-done.5
  97.5 0.0 copy-done.6
  97.5 0.0 copy-done.7
  97.5 0.0 copy-done.8
  97.5 0.0 copy-done.9
  97.5 9.4 %shard_map.139 = bf16[256,2,16,128]{3,2,1,0:T(8,128)(2,1)S(1)} custom-call(bf16[32,8,3,16,128]{4,3,2,1,0:T(8,128)(2,1)S(1)} %bitcast.1, bf16[512,256]{1,0:T(8,128)(2,1)S(1)} %copy-done.5, bf16[256,256]{1,0:T(8,128)(2,1)S(1)} %copy-done.9, bf16[256,256]{1,0:T(8,128)(2,1)S(1)} %copy-done.8, bf16[256,512]{1,0:T(8,128)(2,1)S(1)} %copy-done.4, ...), custom_call_target="tpu_custom_call" | custom-call | tf_op jit(solution)/shard_map/pallas_call | solution.py:164
  107.0 0.0 copy-start
  107.0 0.0 copy-start.1
  107.0 0.0 copy-start.2
  107.0 0.0 copy-start.3
  107.0 59.1 %all_to_all.11.sums = bf16[256,2,16,128]{3,2,1,0:T(8,128)(2,1)S(1)} all-to-all(bf16[256,2,16,128]{3,2,1,0:T(8,128)(2,1)S(1)} %shard_map.139), channel_id=1, replica_groups=mesh['dp'=32,'ctx'=8] {'dp','ctx'}, dimensions={0} | all-to-all | bytes 4194304 | tf_op jit(solution)/shard_map/all_to_all | solution.py:231
  166.1 0.0 copy-done
  166.1 0.0 copy-done.1
  166.1 0.0 copy-done.2
  166.1 0.0 copy-done.3
  166.1 3.5 %shard_map.140 = (bf16[128,4096]{1,0:T(8,128)(2,1)}, bf16[128,4096]{1,0:T(8,128)(2,1)}, bf16[128,4096]{1,0:T(8,128)(2,1)}, bf16[128,4096]{1,0:T(8,128)(2,1)}) custom-call(bf16[256,2,16,128]{3,2,1,0:T(8,128)(2,1)S(1)} %all_to_all.11.sums, bf16[128,4096]{1,0:T(8,128)(2,1)S(1)} %copy-done, bf16[128,4096]{1,0:T(8,128)(2,1)S(1)} %copy-done.1, ...), custom_call_target="tpu_custom_call" | custom-call | tf_op jit(solution)/shard_map/pallas_call | solution.py:210
Async XLA Ops:
  6.4 91.1 %copy-start.4 = (bf16[256,512]{1,0:T(8,128)(2,1)S(1)}, bf16[256,512]{1,0:T(8,128)(2,1)}, u32[]{:S(2)}) copy-start(bf16[256,512]{1,0:T(8,128)(2,1)} %constant.15.clone.outer_bwd) | copy-start | bytes 786436
  6.4 91.0 %copy-start.5 = (bf16[512,256]{1,0:T(8,128)(2,1)S(1)}, bf16[512,256]{1,0:T(8,128)(2,1)}, u32[]{:S(2)}) copy-start(bf16[512,256]{1,0:T(8,128)(2,1)} %constant.12.clone.outer_fwd) | copy-start | bytes 786436
  6.5 91.0 %copy-start.6 = (f32[256,128]{1,0:T(8,128)S(1)}, f32[256,128]{1,0:T(8,128)}, u32[]{:S(2)}) copy-start(f32[256,128]{1,0:T(8,128)} %constant.17.clone.sin) | copy-start | bytes 393220
  6.5 91.0 %copy-start.7 = (f32[256,128]{1,0:T(8,128)S(1)}, f32[256,128]{1,0:T(8,128)}, u32[]{:S(2)}) copy-start(f32[256,128]{1,0:T(8,128)} %constant.16.clone.cos) | copy-start | bytes 393220
  6.5 91.0 %copy-start.8 = (bf16[256,256]{1,0:T(8,128)(2,1)S(1)}, bf16[256,256]{1,0:T(8,128)(2,1)}, u32[]{:S(2)}) copy-start(bf16[256,256]{1,0:T(8,128)(2,1)} %constant.14.clone.inner_bwd) | copy-start | bytes 393220
  6.5 91.0 %copy-start.9 = (bf16[256,256]{1,0:T(8,128)(2,1)S(1)}, bf16[256,256]{1,0:T(8,128)(2,1)}, u32[]{:S(2)}) copy-start(bf16[256,256]{1,0:T(8,128)(2,1)} %constant.13.clone.inner_fwd) | copy-start | bytes 393220
  107.0 59.1 %copy-start = (bf16[128,4096]{1,0:T(8,128)(2,1)S(1)}, bf16[128,4096]{1,0:T(8,128)(2,1)}, u32[]{:S(2)}) copy-start(bf16[128,4096]{1,0:T(8,128)(2,1)} %query.3) | copy-start | bytes 3145732
  107.0 59.1 %copy-start.1 = (bf16[128,4096]{1,0:T(8,128)(2,1)S(1)}, bf16[128,4096]{1,0:T(8,128)(2,1)}, u32[]{:S(2)}) copy-start(bf16[128,4096]{1,0:T(8,128)(2,1)} %key.3) | copy-start | bytes 3145732
  107.0 59.1 %copy-start.2 = (bf16[128,4096]{1,0:T(8,128)(2,1)S(1)}, bf16[128,4096]{1,0:T(8,128)(2,1)}, u32[]{:S(2)}) copy-start(bf16[128,4096]{1,0:T(8,128)(2,1)} %value.3) | copy-start | bytes 3145732
  107.0 59.1 %copy-start.3 = (bf16[128,4096]{1,0:T(8,128)(2,1)S(1)}, bf16[128,4096]{1,0:T(8,128)(2,1)}, u32[]{:S(2)}) copy-start(bf16[128,4096]{1,0:T(8,128)(2,1)} %grad.3) | copy-start | bytes 3145732

commit v3 on v2

--- a/solution.py
+++ b/solution.py
@@ -8,6 +8,8 @@
 from jax.sharding import PartitionSpec as P
 
 LANES = 128
+TILE = 16
+PITCH = 24
 
 
 def tables(length):
@@ -19,12 +21,13 @@
     spin = 2.0 * np.pi / period * np.outer(freq, np.arange(LANES))
     cos, sin = np.cos(inner), np.sin(inner)
     kind = ml_dtypes.bfloat16
-    outer_fwd = np.concatenate([np.cos(outer), -np.sin(outer)], axis=0).astype(kind)
+    both = np.stack([np.cos(outer), -np.sin(outer)], axis=1)
+    both = both.reshape(rows // TILE, TILE, 2, rows).transpose(0, 2, 1, 3).reshape(2 * rows, rows)
+    outer_fwd = both.astype(kind)
     inner_fwd = np.block([[cos, -sin], [sin, cos]]).astype(kind)
     inner_bwd = np.block([[cos, sin], [-sin, cos]]).astype(kind)
     scale = np.float32(2.0 / period)
-    outer_bwd = np.concatenate([np.cos(outer).T, -np.sin(outer).T], axis=1).astype(kind)
-    outer_bwd = (outer_bwd.astype(np.float32) * scale).astype(kind)
+    outer_bwd = (both.T.astype(kind).astype(np.float32) * scale).astype(kind)
     spin_cos = np.cos(spin).astype(np.float32)
     spin_sin = np.sin(spin).astype(np.float32)
     return outer_fwd, inner_fwd, inner_bwd, outer_bwd, spin_cos, spin_sin
@@ -43,8 +46,9 @@
 
     def send(slot, first, count):
         some = slice(first, first + count)
-        lines = spread[slot, first * per_owner : (first + count) * per_owner]
-        ready[slot, some] = lines.reshape(count, per_owner, LANES).astype(jnp.bfloat16)
+        lines = spread[slot, first * PITCH : (first + count) * PITCH]
+        lines = lines.reshape(count, PITCH, LANES)[:, :per_owner]
+        ready[slot, some] = lines.astype(jnp.bfloat16)
         stores.append(
             pltpu.make_async_copy(
                 ready.at[slot, some], out.at[some, slot], out_sems.at[len(stores)]
@@ -56,7 +60,7 @@
     for j in range(2):
         for a in range(half):
             lines = raw_filt[a * LANES : (a + 1) * LANES, j * owners : (j + 1) * owners]
-            spread[2, pl.ds(j * half + a, owners, stride=per_owner), :] = lines.astype(jnp.float32).T
+            spread[2, pl.ds(j * half + a, owners, stride=PITCH), :] = lines.astype(jnp.float32).T
     send(2, 0, owners)
     for slot in range(2):
         loads[2 * slot].wait()
@@ -66,7 +70,7 @@
             prod = raw[2 * slot, :, columns].astype(jnp.float32) * raw[
                 2 * slot + 1, :, columns
             ].astype(jnp.float32)
-            spread[slot, pl.ds(i, owners, stride=per_owner), :] = prod.T
+            spread[slot, pl.ds(i, owners, stride=PITCH), :] = prod.T
         if slot == 0:
             send(slot, 0, owners)
         else:
@@ -87,7 +91,7 @@
         scratch_shapes=[
             pltpu.VMEM((4, tokens, channels), jnp.bfloat16),
             pltpu.VMEM(filt.shape, jnp.bfloat16),
-            pltpu.VMEM((3, owners * per_owner, LANES), jnp.float32),
+            pltpu.VMEM((3, owners * PITCH, LANES), jnp.float32),
             pltpu.VMEM((3, owners, per_owner, LANES), jnp.bfloat16),
             pltpu.SemaphoreType.DMA((5,)),
             pltpu.SemaphoreType.DMA((6,)),
@@ -101,9 +105,11 @@
     rows = blocks_p * groups
     half = per_owner // 2
     for slot in range(2):
-        wide[slot] = (
-            blocks[:, :, slot].astype(jnp.float32).reshape(rows * per_owner, LANES)
-        )
+        lines = blocks[:, :, slot].astype(jnp.float32).reshape(rows, per_owner, LANES)
+        wide[slot, :, :per_owner] = lines
+
+    wide = wide.reshape(2, rows * PITCH, LANES)
+    flat = done.reshape(2, rows * PITCH, LANES)
 
     def dot(left, right):
         return jnp.dot(left, right, preferred_element_type=jnp.float32)
@@ -113,20 +119,23 @@
         lines = [filt[:, j * half : (j + 1) * half].reshape(rows, LANES) for j in range(2)]
         for slot in range(2):
             for j in range(2):
-                lines.append(wide[slot, pl.ds(2 * group + j, rows, stride=per_owner), :])
-        mid = dot(outer_fwd[...], jnp.concatenate(lines, axis=1).astype(jnp.bfloat16))
+                lines.append(wide[slot, pl.ds(2 * group + j, rows, stride=PITCH), :])
+        mids = []
+        for i in range(3):
+            pair = jnp.concatenate(lines[2 * i : 2 * i + 2], axis=1).astype(jnp.bfloat16)
+            mid = dot(outer_fwd[...], pair).reshape(rows // TILE, 2, TILE, 2 * LANES)
+            mids += [mid[..., :LANES], mid[..., LANES:]]
+        c, s = cos[...].reshape(rows // TILE, TILE, LANES), sin[...].reshape(rows // TILE, TILE, LANES)
         spun = []
-        for i in range(6):
-            real = mid[:rows, i * LANES : (i + 1) * LANES]
-            imag = mid[rows:, i * LANES : (i + 1) * LANES]
+        for mid in mids:
+            real, imag = mid[:, 0], mid[:, 1]
             spun.append(jnp.concatenate(
-                [real * cos[...] + imag * sin[...], imag * cos[...] - real * sin[...]], axis=1
-            ).astype(jnp.bfloat16))
-        both = dot(jnp.concatenate(spun, axis=0), inner_fwd[...])
-        spec = [
-            (both[i * rows : (i + 1) * rows, :LANES], both[i * rows : (i + 1) * rows, LANES:])
-            for i in range(6)
-        ]
+                [real * c + imag * s, imag * c - real * s], axis=2
+            ).reshape(rows, 2 * LANES).astype(jnp.bfloat16))
+        spec = []
+        for i in range(3):
+            both = dot(jnp.concatenate(spun[2 * i : 2 * i + 2], axis=0), inner_fwd[...])
+            spec += [(both[:rows, :LANES], both[:rows, LANES:]), (both[rows:, :LANES], both[rows:, LANES:])]
         mixed = []
         for slot in range(2):
             for j in range(2):
@@ -136,26 +145,25 @@
                 else:
                     real, imag = fr * gr + fi * gi, fr * gi - fi * gr
                 mixed.append(jnp.concatenate([real, imag], axis=1).astype(jnp.bfloat16))
-        both = dot(jnp.concatenate(mixed, axis=0), inner_bwd[...])
+        boths = [dot(m, inner_bwd[...]) for m in mixed]
         spun = []
-        for i in range(4):
-            real = both[i * rows : (i + 1) * rows, :LANES]
-            imag = both[i * rows : (i + 1) * rows, LANES:]
-            spun.append(jnp.concatenate(
-                [real * cos[...] - imag * sin[...], real * sin[...] + imag * cos[...]], axis=0
-            ).astype(jnp.bfloat16))
-        result = dot(outer_bwd[...], jnp.concatenate(spun, axis=1))
+        for both in boths:
+            both = both.reshape(rows // TILE, TILE, 2 * LANES)
+            real, imag = both[..., :LANES], both[..., LANES:]
+            spun.append(jnp.stack(
+                [real * c - imag * s, real * s + imag * c], axis=1
+            ).reshape(2 * rows, LANES).astype(jnp.bfloat16))
         for slot in range(2):
-            for j in range(2):
-                i = 2 * slot + j
-                done[slot, pl.ds(2 * group + j, rows, stride=per_owner), :] = result[
-                    :, i * LANES : (i + 1) * LANES
+            result = dot(outer_bwd[...], jnp.concatenate(spun[2 * slot : 2 * slot + 2], axis=1))
+            for j in range(2):
+                flat[slot, pl.ds(2 * group + j, rows, stride=PITCH), :] = result[
+                    :, j * LANES : (j + 1) * LANES
                 ]
         return carry
 
     lax.fori_loop(0, groups, step, 0, unroll=True)
     for slot in range(2):
-        out[:, slot] = done[slot].reshape(rows, per_owner, LANES).astype(jnp.bfloat16)
+        out[:, slot] = done[slot, :, :per_owner].astype(jnp.bfloat16)
 
 
 def mix(blocks, groups):
@@ -165,10 +173,10 @@
         mix_kernel,
         out_shape=jax.ShapeDtypeStruct((rows, 2, per_owner, LANES), jnp.bfloat16),
         scratch_shapes=[
-            pltpu.VMEM((2, rows * per_owner, LANES), jnp.float32),
-            pltpu.VMEM((2, rows * per_owner, LANES), jnp.float32),
+            pltpu.VMEM((2, rows, PITCH, LANES), jnp.float32),
+            pltpu.VMEM((2, rows, PITCH, LANES), jnp.float32),
         ],
-        compiler_params=pltpu.CompilerParams(vmem_limit_bytes=24 << 20),
+        compiler_params=pltpu.CompilerParams(vmem_limit_bytes=32 << 20),
     )(blocks.reshape(rows // groups, groups, 3, per_owner, LANES), *consts)
 
 
@@ -178,13 +186,14 @@
     width = 2 * owners
     uses = ((query, gated), (grad, grad_query)), ((value, grad_key), (key, grad_value))
     stores = []
-    for slot in range(2):
-        wide[slot] = sums[:, slot].astype(jnp.float32).reshape(owners * per_owner, LANES)
+    flat = wide.reshape(2, owners * PITCH, LANES)
+    for slot in range(2):
+        wide[slot, :, :per_owner] = sums[:, slot].astype(jnp.float32)
         for group in range(channels // width):
             for j in range(2):
                 i = 2 * group + j
                 columns = slice(i * owners, (i + 1) * owners)
-                tokens = wide[slot, pl.ds(i, owners, stride=per_owner), :].T
+                tokens = flat[slot, pl.ds(i, owners, stride=PITCH), :].T
                 for k, (source, _) in enumerate(uses[slot]):
                     ready[2 * slot + k, :, columns] = (
                         source[:, columns].astype(jnp.float32) * tokens
@@ -213,7 +222,7 @@
         out_specs=[pl.BlockSpec(memory_space=pltpu.HBM)] * 4,
         out_shape=[jax.ShapeDtypeStruct((tokens, channels), jnp.bfloat16)] * 4,
         scratch_shapes=[
-            pltpu.VMEM((2, owners * per_owner, LANES), jnp.float32),
+            pltpu.VMEM((2, owners, PITCH, LANES), jnp.float32),
             pltpu.VMEM((4, tokens, channels), jnp.bfloat16),
             pltpu.SemaphoreType.DMA((4 * channels // width,)),
         ],

time: 170 us -> 165 us (0.971)
  Pallas kernels: 18.7 us -> 14.2 us
    pallas_call x1, Pallas kernels: 9.42 us -> 6.89 us  [mix(): pl.pallas_call(mix_kernel, out_shape=jax.ShapeDtypeStruct((rows, 2, per_o...]
where the time goes in v3:
time: 165 us
  blocking collectives  150 us (91%)
  Pallas kernels  14.2 us (9%)
    all_to_all x1, blocking collectives, body(): lax.all_to_all(packed, axes, split_axis=0, concat_axis=0, tiled=True)  91 us
    all_to_all x1, blocking collectives, body(): sums = lax.all_to_all(mixed, axes, split_axis=0, concat_axis=0, tiled=True)  59.1 us
    pallas_call x1, Pallas kernels, mix(): pl.pallas_call(mix_kernel, out_shape=jax.ShapeDtypeStruct((rows, 2, per_o...  6.89 us
    pallas_call x1, Pallas kernels, pack(): pl.pallas_call(pack_kernel, in_specs=[pl.BlockSpec(memory_space=pltpu.HBM...  4.56 us

profile of v3, /device:TPU:1, one launch (start us, length us, event | category | flops | bytes accessed | tf_op | source)
XLA Modules:
  0.0 165.1 jit_solution(16989800410301637878)
XLA Ops:
  0.6 4.6 %shard_map.138 = bf16[256,3,16,128]{3,2,1,0:T(8,128)(2,1)} custom-call(bf16[128,4096]{1,0:T(8,128)(2,1)} %query.3, bf16[128,4096]{1,0:T(8,128)(2,1)} %key.3, bf16[128,4096]{1,0:T(8,128)(2,1)} %value.3, bf16[128,4096]{1,0:T(8,128)(2,1)} %grad.3, bf16[1024,512]{1,0:T(8,128)(2,1)} %filt.1), custom_call_target="tpu_custom_call" | custom-call | tf_op jit(solution)/shard_map/pallas_call | solution.py:86
  5.2 0.0 copy-start.4
  5.2 0.0 copy-start.5
  5.2 0.0 copy-start.6
  5.2 0.0 copy-start.7
  5.2 0.0 copy-start.8
  5.3 0.0 copy-start.9
  5.3 91.0 %all_to_all.10 = bf16[256,3,16,128]{3,2,1,0:T(8,128)(2,1)S(1)} all-to-all(bf16[256,3,16,128]{3,2,1,0:T(8,128)(2,1)} %shard_map.138), channel_id=1, replica_groups=mesh['dp'=32,'ctx'=8] {'dp','ctx'}, dimensions={0} | all-to-all | bytes 6291456 | tf_op jit(solution)/shard_map/all_to_all | solution.py:238
  96.2 0.0 copy-done.4
  96.3 0.0 copy-done.5
  96.3 0.0 copy-done.6
  96.3 0.0 copy-done.7
  96.3 0.0 copy-done.8
  96.3 0.0 copy-done.9
  96.3 6.9 %shard_map.139 = bf16[256,2,16,128]{3,2,1,0:T(8,128)(2,1)S(1)} custom-call(bf16[32,8,3,16,128]{4,3,2,1,0:T(8,128)(2,1)S(1)} %bitcast.1, bf16[512,256]{1,0:T(8,128)(2,1)S(1)} %copy-done.5, bf16[256,256]{1,0:T(8,128)(2,1)S(1)} %copy-done.9, bf16[256,256]{1,0:T(8,128)(2,1)S(1)} %copy-done.8, bf16[256,512]{1,0:T(8,128)(2,1)S(1)} %copy-done.4, ...), custom_call_target="tpu_custom_call" | custom-call | tf_op jit(solution)/shard_map/pallas_call | solution.py:172
  103.2 0.0 copy-start
  103.2 0.0 copy-start.1
  103.2 0.0 copy-start.2
  103.2 0.0 copy-start.3
  103.2 59.1 %all_to_all.11.sums = bf16[256,2,16,128]{3,2,1,0:T(8,128)(2,1)S(1)} all-to-all(bf16[256,2,16,128]{3,2,1,0:T(8,128)(2,1)S(1)} %shard_map.139), channel_id=1, replica_groups=mesh['dp'=32,'ctx'=8] {'dp','ctx'}, dimensions={0} | all-to-all | bytes 4194304 | tf_op jit(solution)/shard_map/all_to_all | solution.py:240
  162.3 0.0 copy-done
  162.3 0.0 copy-done.1
  162.3 0.0 copy-done.2
  162.3 0.0 copy-done.3
  162.4 2.7 %shard_map.140 = (bf16[128,4096]{1,0:T(8,128)(2,1)}, bf16[128,4096]{1,0:T(8,128)(2,1)}, bf16[128,4096]{1,0:T(8,128)(2,1)}, bf16[128,4096]{1,0:T(8,128)(2,1)}) custom-call(bf16[256,2,16,128]{3,2,1,0:T(8,128)(2,1)S(1)} %all_to_all.11.sums, bf16[128,4096]{1,0:T(8,128)(2,1)S(1)} %copy-done, bf16[128,4096]{1,0:T(8,128)(2,1)S(1)} %copy-done.1, ...), custom_call_target="tpu_custom_call" | custom-call | tf_op jit(solution)/shard_map/pallas_call | solution.py:219
Async XLA Ops:
  5.2 91.1 %copy-start.4 = (bf16[256,512]{1,0:T(8,128)(2,1)S(1)}, bf16[256,512]{1,0:T(8,128)(2,1)}, u32[]{:S(2)}) copy-start(bf16[256,512]{1,0:T(8,128)(2,1)} %constant.15.clone.outer_bwd) | copy-start | bytes 786436
  5.2 91.0 %copy-start.5 = (bf16[512,256]{1,0:T(8,128)(2,1)S(1)}, bf16[512,256]{1,0:T(8,128)(2,1)}, u32[]{:S(2)}) copy-start(bf16[512,256]{1,0:T(8,128)(2,1)} %constant.12.clone.outer_fwd) | copy-start | bytes 786436
  5.2 91.0 %copy-start.6 = (f32[256,128]{1,0:T(8,128)S(1)}, f32[256,128]{1,0:T(8,128)}, u32[]{:S(2)}) copy-start(f32[256,128]{1,0:T(8,128)} %constant.17.clone.sin) | copy-start | bytes 393220
  5.2 91.0 %copy-start.7 = (f32[256,128]{1,0:T(8,128)S(1)}, f32[256,128]{1,0:T(8,128)}, u32[]{:S(2)}) copy-start(f32[256,128]{1,0:T(8,128)} %constant.16.clone.cos) | copy-start | bytes 393220
  5.2 91.0 %copy-start.8 = (bf16[256,256]{1,0:T(8,128)(2,1)S(1)}, bf16[256,256]{1,0:T(8,128)(2,1)}, u32[]{:S(2)}) copy-start(bf16[256,256]{1,0:T(8,128)(2,1)} %constant.14.clone.inner_bwd) | copy-start | bytes 393220
  5.3 91.0 %copy-start.9 = (bf16[256,256]{1,0:T(8,128)(2,1)S(1)}, bf16[256,256]{1,0:T(8,128)(2,1)}, u32[]{:S(2)}) copy-start(bf16[256,256]{1,0:T(8,128)(2,1)} %constant.13.clone.inner_fwd) | copy-start | bytes 393220
  103.2 59.2 %copy-start = (bf16[128,4096]{1,0:T(8,128)(2,1)S(1)}, bf16[128,4096]{1,0:T(8,128)(2,1)}, u32[]{:S(2)}) copy-start(bf16[128,4096]{1,0:T(8,128)(2,1)} %query.3) | copy-start | bytes 3145732
  103.2 59.1 %copy-start.1 = (bf16[128,4096]{1,0:T(8,128)(2,1)S(1)}, bf16[128,4096]{1,0:T(8,128)(2,1)}, u32[]{:S(2)}) copy-start(bf16[128,4096]{1,0:T(8,128)(2,1)} %key.3) | copy-start | bytes 3145732
  103.2 59.1 %copy-start.2 = (bf16[128,4096]{1,0:T(8,128)(2,1)S(1)}, bf16[128,4096]{1,0:T(8,128)(2,1)}, u32[]{:S(2)}) copy-start(bf16[128,4096]{1,0:T(8,128)(2,1)} %value.3) | copy-start | bytes 3145732
  103.2 59.1 %copy-start.3 = (bf16[128,4096]{1,0:T(8,128)(2,1)S(1)}, bf16[128,4096]{1,0:T(8,128)(2,1)}, u32[]{:S(2)}) copy-start(bf16[128,4096]{1,0:T(8,128)(2,1)} %grad.3) | copy-start | bytes 3145732

commit v4 on v3

--- a/solution.py
+++ b/solution.py
@@ -33,7 +33,7 @@
     return outer_fwd, inner_fwd, inner_bwd, outer_bwd, spin_cos, spin_sin
 
 
-def pack_kernel(query, key, value, grad, filt, out, raw, raw_filt, spread, ready, sems, out_sems):
+def pack_kernel(query, key, value, grad, filt, out, raw, raw_filt, spread, sems):
     owners, _, per_owner, _ = out.shape
     half = per_owner // 2
     load_filt = pltpu.make_async_copy(filt, raw_filt, sems.at[4])
@@ -42,19 +42,12 @@
     for i, source in enumerate((key, value, grad, query)):
         loads.append(pltpu.make_async_copy(source, raw.at[i], sems.at[i]))
         loads[-1].start()
-    stores = []
 
     def send(slot, first, count):
         some = slice(first, first + count)
         lines = spread[slot, first * PITCH : (first + count) * PITCH]
         lines = lines.reshape(count, PITCH, LANES)[:, :per_owner]
-        ready[slot, some] = lines.astype(jnp.bfloat16)
-        stores.append(
-            pltpu.make_async_copy(
-                ready.at[slot, some], out.at[some, slot], out_sems.at[len(stores)]
-            )
-        )
-        stores[-1].start()
+        out[some, slot] = lines.astype(jnp.bfloat16)
 
     load_filt.wait()
     for j in range(2):
@@ -71,13 +64,7 @@
                 2 * slot + 1, :, columns
             ].astype(jnp.float32)
             spread[slot, pl.ds(i, owners, stride=PITCH), :] = prod.T
-        if slot == 0:
-            send(slot, 0, owners)
-        else:
-            for part in range(4):
-                send(slot, part * (owners // 4), owners // 4)
-    for store in stores:
-        store.wait()
+        send(slot, 0, owners)
 
 
 def pack(query, key, value, grad, filt, owners):
@@ -86,18 +73,16 @@
     return pl.pallas_call(
         pack_kernel,
         in_specs=[pl.BlockSpec(memory_space=pltpu.HBM)] * 5,
-        out_specs=pl.BlockSpec(memory_space=pltpu.HBM),
+        out_specs=pl.BlockSpec(memory_space=pltpu.VMEM),
         out_shape=jax.ShapeDtypeStruct((owners, 3, per_owner, LANES), jnp.bfloat16),
         scratch_shapes=[
             pltpu.VMEM((4, tokens, channels), jnp.bfloat16),
             pltpu.VMEM(filt.shape, jnp.bfloat16),
             pltpu.VMEM((3, owners * PITCH, LANES), jnp.float32),
-            pltpu.VMEM((3, owners, per_owner, LANES), jnp.bfloat16),
             pltpu.SemaphoreType.DMA((5,)),
-            pltpu.SemaphoreType.DMA((6,)),
         ],
-        compiler_params=pltpu.CompilerParams(vmem_limit_bytes=60 << 20),
-    )(query, key, value, grad, filt)
+        compiler_params=pltpu.CompilerParams(vmem_limit_bytes=24 << 20),
+    )(*[pltpu.with_memory_space_constraint(x, pltpu.HBM) for x in (query, key, value, grad, filt)])
 
 
 def mix_kernel(blocks, outer_fwd, inner_fwd, inner_bwd, outer_bwd, cos, sin, out, wide, done):

time: 165 us -> 164 us (level)
  no operation moved by 1% of the time
where the time goes in v4:
time: 164 us
  blocking collectives  150 us (91%)
  Pallas kernels  13.1 us (8%)
    all_to_all x1, blocking collectives, body(): lax.all_to_all(packed, axes, split_axis=0, concat_axis=0, tiled=True)  90.8 us
    all_to_all x1, blocking collectives, body(): sums = lax.all_to_all(mixed, axes, split_axis=0, concat_axis=0, tiled=True)  59.1 us
    pallas_call x1, Pallas kernels, mix(): pl.pallas_call(mix_kernel, out_shape=jax.ShapeDtypeStruct((rows, 2, per_o...  6.89 us
    pallas_call x1, Pallas kernels, pack(): pl.pallas_call(pack_kernel, in_specs=[pl.BlockSpec(memory_space=pltpu.HBM...  3.5 us

profile of v4, /device:TPU:1, one launch (start us, length us, event | category | flops | bytes accessed | tf_op | source)
XLA Modules:
  0.0 163.8 jit_solution(14730052565847954469)
XLA Ops:
  0.6 3.5 %shard_map.138 = bf16[256,3,16,128]{3,2,1,0:T(8,128)(2,1)S(1)} custom-call(bf16[128,4096]{1,0:T(8,128)(2,1)} %query.3, bf16[128,4096]{1,0:T(8,128)(2,1)} %key.3, bf16[128,4096]{1,0:T(8,128)(2,1)} %value.3, bf16[128,4096]{1,0:T(8,128)(2,1)} %grad.3, bf16[1024,512]{1,0:T(8,128)(2,1)} %filt.1), custom_call_target="tpu_custom_call" | custom-call | tf_op jit(solution)/shard_map/pallas_call | solution.py:73
  4.1 0.0 copy-start.4
  4.2 0.0 copy-start.5
  4.2 0.0 copy-start.6
  4.2 0.0 copy-start.7
  4.2 0.0 copy-start.8
  4.2 0.0 copy-start.9
  4.2 90.8 %all_to_all.10 = bf16[256,3,16,128]{3,2,1,0:T(8,128)(2,1)S(1)} all-to-all(bf16[256,3,16,128]{3,2,1,0:T(8,128)(2,1)S(1)} %shard_map.138), channel_id=1, replica_groups=mesh['dp'=32,'ctx'=8] {'dp','ctx'}, dimensions={0} | all-to-all | bytes 6291456 | tf_op jit(solution)/shard_map/all_to_all | solution.py:223
  95.0 0.0 copy-done.4
  95.0 0.0 copy-done.5
  95.0 0.0 copy-done.6
  95.0 0.0 copy-done.7
  95.0 0.0 copy-done.8
  95.0 0.0 copy-done.9
  95.0 6.9 %shard_map.139 = bf16[256,2,16,128]{3,2,1,0:T(8,128)(2,1)S(1)} custom-call(bf16[32,8,3,16,128]{4,3,2,1,0:T(8,128)(2,1)S(1)} %bitcast.1, bf16[512,256]{1,0:T(8,128)(2,1)S(1)} %copy-done.5, bf16[256,256]{1,0:T(8,128)(2,1)S(1)} %copy-done.9, bf16[256,256]{1,0:T(8,128)(2,1)S(1)} %copy-done.8, bf16[256,512]{1,0:T(8,128)(2,1)S(1)} %copy-done.4, ...), custom_call_target="tpu_custom_call" | custom-call | tf_op jit(solution)/shard_map/pallas_call | solution.py:157
  101.9 0.0 copy-start
  101.9 0.0 copy-start.1
  101.9 0.0 copy-start.2
  102.0 0.0 copy-start.3
  102.0 59.1 %all_to_all.11.sums = bf16[256,2,16,128]{3,2,1,0:T(8,128)(2,1)S(1)} all-to-all(bf16[256,2,16,128]{3,2,1,0:T(8,128)(2,1)S(1)} %shard_map.139), channel_id=1, replica_groups=mesh['dp'=32,'ctx'=8] {'dp','ctx'}, dimensions={0} | all-to-all | bytes 4194304 | tf_op jit(solution)/shard_map/all_to_all | solution.py:225
  161.1 0.0 copy-done
  161.1 0.0 copy-done.1
  161.1 0.0 copy-done.2
  161.1 0.0 copy-done.3
  161.1 2.7 %shard_map.140 = (bf16[128,4096]{1,0:T(8,128)(2,1)}, bf16[128,4096]{1,0:T(8,128)(2,1)}, bf16[128,4096]{1,0:T(8,128)(2,1)}, bf16[128,4096]{1,0:T(8,128)(2,1)}) custom-call(bf16[256,2,16,128]{3,2,1,0:T(8,128)(2,1)S(1)} %all_to_all.11.sums, bf16[128,4096]{1,0:T(8,128)(2,1)S(1)} %copy-done, bf16[128,4096]{1,0:T(8,128)(2,1)S(1)} %copy-done.1, ...), custom_call_target="tpu_custom_call" | custom-call | tf_op jit(solution)/shard_map/pallas_call | solution.py:204
Async XLA Ops:
  4.1 90.8 %copy-start.4 = (bf16[256,512]{1,0:T(8,128)(2,1)S(1)}, bf16[256,512]{1,0:T(8,128)(2,1)}, u32[]{:S(2)}) copy-start(bf16[256,512]{1,0:T(8,128)(2,1)} %constant.15.clone.outer_bwd) | copy-start | bytes 786436
  4.2 90.8 %copy-start.5 = (bf16[512,256]{1,0:T(8,128)(2,1)S(1)}, bf16[512,256]{1,0:T(8,128)(2,1)}, u32[]{:S(2)}) copy-start(bf16[512,256]{1,0:T(8,128)(2,1)} %constant.12.clone.outer_fwd) | copy-start | bytes 786436
  4.2 90.8 %copy-start.6 = (f32[256,128]{1,0:T(8,128)S(1)}, f32[256,128]{1,0:T(8,128)}, u32[]{:S(2)}) copy-start(f32[256,128]{1,0:T(8,128)} %constant.17.clone.sin) | copy-start | bytes 393220
  4.2 90.8 %copy-start.7 = (f32[256,128]{1,0:T(8,128)S(1)}, f32[256,128]{1,0:T(8,128)}, u32[]{:S(2)}) copy-start(f32[256,128]{1,0:T(8,128)} %constant.16.clone.cos) | copy-start | bytes 393220
  4.2 90.8 %copy-start.8 = (bf16[256,256]{1,0:T(8,128)(2,1)S(1)}, bf16[256,256]{1,0:T(8,128)(2,1)}, u32[]{:S(2)}) copy-start(bf16[256,256]{1,0:T(8,128)(2,1)} %constant.14.clone.inner_bwd) | copy-start | bytes 393220
  4.2 90.8 %copy-start.9 = (bf16[256,256]{1,0:T(8,128)(2,1)S(1)}, bf16[256,256]{1,0:T(8,128)(2,1)}, u32[]{:S(2)}) copy-start(bf16[256,256]{1,0:T(8,128)(2,1)} %constant.13.clone.inner_fwd) | copy-start | bytes 393220
  101.9 59.2 %copy-start = (bf16[128,4096]{1,0:T(8,128)(2,1)S(1)}, bf16[128,4096]{1,0:T(8,128)(2,1)}, u32[]{:S(2)}) copy-start(bf16[128,4096]{1,0:T(8,128)(2,1)} %query.3) | copy-start | bytes 3145732
  101.9 59.1 %copy-start.1 = (bf16[128,4096]{1,0:T(8,128)(2,1)S(1)}, bf16[128,4096]{1,0:T(8,128)(2,1)}, u32[]{:S(2)}) copy-start(bf16[128,4096]{1,0:T(8,128)(2,1)} %key.3) | copy-start | bytes 3145732
  101.9 59.1 %copy-start.2 = (bf16[128,4096]{1,0:T(8,128)(2,1)S(1)}, bf16[128,4096]{1,0:T(8,128)(2,1)}, u32[]{:S(2)}) copy-start(bf16[128,4096]{1,0:T(8,128)(2,1)} %value.3) | copy-start | bytes 3145732
  102.0 59.1 %copy-start.3 = (bf16[128,4096]{1,0:T(8,128)(2,1)S(1)}, bf16[128,4096]{1,0:T(8,128)(2,1)}, u32[]{:S(2)}) copy-start(bf16[128,4096]{1,0:T(8,128)(2,1)} %grad.3) | copy-start | bytes 3145732

commit v5 on v4

--- a/solution.py
+++ b/solution.py
@@ -33,6 +33,17 @@
     return outer_fwd, inner_fwd, inner_bwd, outer_bwd, spin_cos, spin_sin
 
 
+def turned(block):
+    size = block.shape[0]
+    eye = (
+        lax.broadcasted_iota(jnp.int32, (size, size), 0)
+        == lax.broadcasted_iota(jnp.int32, (size, size), 1)
+    ).astype(jnp.bfloat16)
+    return lax.dot_general(
+        block, eye, (((0,), (0,)), ((), ())), preferred_element_type=jnp.float32
+    )
+
+
 def pack_kernel(query, key, value, grad, filt, out, raw, raw_filt, spread, sems):
     owners, _, per_owner, _ = out.shape
     half = per_owner // 2
@@ -53,7 +64,7 @@
     for j in range(2):
         for a in range(half):
             lines = raw_filt[a * LANES : (a + 1) * LANES, j * owners : (j + 1) * owners]
-            spread[2, pl.ds(j * half + a, owners, stride=PITCH), :] = lines.astype(jnp.float32).T
+            spread[2, pl.ds(j * half + a, owners, stride=PITCH), :] = turned(lines)
     send(2, 0, owners)
     for slot in range(2):
         loads[2 * slot].wait()
@@ -63,7 +74,7 @@
             prod = raw[2 * slot, :, columns].astype(jnp.float32) * raw[
                 2 * slot + 1, :, columns
             ].astype(jnp.float32)
-            spread[slot, pl.ds(i, owners, stride=PITCH), :] = prod.T
+            spread[slot, pl.ds(i, owners, stride=PITCH), :] = turned(prod.astype(jnp.bfloat16))
         send(slot, 0, owners)
 
 
@@ -78,7 +89,7 @@
         scratch_shapes=[
             pltpu.VMEM((4, tokens, channels), jnp.bfloat16),
             pltpu.VMEM(filt.shape, jnp.bfloat16),
-            pltpu.VMEM((3, owners * PITCH, LANES), jnp.float32),
+            pltpu.VMEM((3, (owners + 1) * PITCH, LANES), jnp.float32),
             pltpu.SemaphoreType.DMA((5,)),
         ],
         compiler_params=pltpu.CompilerParams(vmem_limit_bytes=24 << 20),
@@ -91,64 +102,70 @@
     half = per_owner // 2
     for slot in range(2):
         lines = blocks[:, :, slot].astype(jnp.float32).reshape(rows, per_owner, LANES)
-        wide[slot, :, :per_owner] = lines
-
-    wide = wide.reshape(2, rows * PITCH, LANES)
-    flat = done.reshape(2, rows * PITCH, LANES)
+        wide[slot, :rows, :per_owner] = lines
+
+    wide = wide.reshape(2, (rows + 1) * PITCH, LANES)
+    flat = done.reshape(2, (rows + 1) * PITCH, LANES)
 
     def dot(left, right):
         return jnp.dot(left, right, preferred_element_type=jnp.float32)
 
     def step(group, carry):
+        c, s = cos[...].reshape(rows // TILE, TILE, LANES), sin[...].reshape(rows // TILE, TILE, LANES)
         filt = blocks[:, group, 2].astype(jnp.float32)
         lines = [filt[:, j * half : (j + 1) * half].reshape(rows, LANES) for j in range(2)]
         for slot in range(2):
             for j in range(2):
                 lines.append(wide[slot, pl.ds(2 * group + j, rows, stride=PITCH), :])
-        mids = []
-        for i in range(3):
-            pair = jnp.concatenate(lines[2 * i : 2 * i + 2], axis=1).astype(jnp.bfloat16)
-            mid = dot(outer_fwd[...], pair).reshape(rows // TILE, 2, TILE, 2 * LANES)
-            mids += [mid[..., :LANES], mid[..., LANES:]]
-        c, s = cos[...].reshape(rows // TILE, TILE, LANES), sin[...].reshape(rows // TILE, TILE, LANES)
-        spun = []
-        for mid in mids:
+
+        def spin(mid):
             real, imag = mid[:, 0], mid[:, 1]
-            spun.append(jnp.concatenate(
+            return jnp.concatenate(
                 [real * c + imag * s, imag * c - real * s], axis=2
-            ).reshape(rows, 2 * LANES).astype(jnp.bfloat16))
-        spec = []
-        for i in range(3):
-            both = dot(jnp.concatenate(spun[2 * i : 2 * i + 2], axis=0), inner_fwd[...])
-            spec += [(both[:rows, :LANES], both[:rows, LANES:]), (both[rows:, :LANES], both[rows:, LANES:])]
-        mixed = []
-        for slot in range(2):
-            for j in range(2):
-                (fr, fi), (gr, gi) = spec[j], spec[2 + 2 * slot + j]
-                if slot == 0:
-                    real, imag = fr * gr - fi * gi, fr * gi + fi * gr
-                else:
-                    real, imag = fr * gr + fi * gi, fr * gi - fi * gr
-                mixed.append(jnp.concatenate([real, imag], axis=1).astype(jnp.bfloat16))
-        boths = [dot(m, inner_bwd[...]) for m in mixed]
-        spun = []
-        for both in boths:
+            ).reshape(rows, 2 * LANES).astype(jnp.bfloat16)
+
+        def back(both):
             both = both.reshape(rows // TILE, TILE, 2 * LANES)
             real, imag = both[..., :LANES], both[..., LANES:]
-            spun.append(jnp.stack(
+            return jnp.stack(
                 [real * c - imag * s, real * s + imag * c], axis=1
-            ).reshape(2 * rows, LANES).astype(jnp.bfloat16))
-        for slot in range(2):
-            result = dot(outer_bwd[...], jnp.concatenate(spun[2 * slot : 2 * slot + 2], axis=1))
+            ).reshape(2 * rows, LANES).astype(jnp.bfloat16)
+
+        def times(slot, j):
+            (fr, fi), (gr, gi) = spec[j], spec[2 + 2 * slot + j]
+            if slot == 0:
+                real, imag = fr * gr - fi * gi, fr * gi + fi * gr
+            else:
+                real, imag = fr * gr + fi * gi, fr * gi - fi * gr
+            return jnp.concatenate([real, imag], axis=1).astype(jnp.bfloat16)
+
+        def finish(slot, spun):
+            result = dot(outer_bwd[...], jnp.concatenate(spun, axis=1))
             for j in range(2):
                 flat[slot, pl.ds(2 * group + j, rows, stride=PITCH), :] = result[
                     :, j * LANES : (j + 1) * LANES
                 ]
+
+        mids, spun, spec = {}, {}, {}
+        for i in (0, 1, 2):
+            pair = jnp.concatenate(lines[2 * i : 2 * i + 2], axis=1).astype(jnp.bfloat16)
+            mid = dot(outer_fwd[...], pair).reshape(rows // TILE, 2, TILE, 2 * LANES)
+            mids[2 * i], mids[2 * i + 1] = mid[..., :LANES], mid[..., LANES:]
+        for i in (0, 1, 2):
+            spun[2 * i], spun[2 * i + 1] = spin(mids[2 * i]), spin(mids[2 * i + 1])
+        for i in (0, 1, 2):
+            both = dot(jnp.concatenate([spun[2 * i], spun[2 * i + 1]], axis=0), inner_fwd[...])
+            spec[2 * i] = both[:rows, :LANES], both[:rows, LANES:]
+            spec[2 * i + 1] = both[rows:, :LANES], both[rows:, LANES:]
+        mixed = [times(slot, j) for slot in range(2) for j in range(2)]
+        boths = [dot(part, inner_bwd[...]) for part in mixed]
+        for slot in range(2):
+            finish(slot, [back(boths[2 * slot]), back(boths[2 * slot + 1])])
         return carry
 
     lax.fori_loop(0, groups, step, 0, unroll=True)
     for slot in range(2):
-        out[:, slot] = done[slot, :, :per_owner].astype(jnp.bfloat16)
+        out[:, slot] = done[slot, :rows, :per_owner].astype(jnp.bfloat16)
 
 
 def mix(blocks, groups):
@@ -158,8 +175,8 @@
         mix_kernel,
         out_shape=jax.ShapeDtypeStruct((rows, 2, per_owner, LANES), jnp.bfloat16),
         scratch_shapes=[
-            pltpu.VMEM((2, rows, PITCH, LANES), jnp.float32),
-            pltpu.VMEM((2, rows, PITCH, LANES), jnp.float32),
+            pltpu.VMEM((2, rows + 1, PITCH, LANES), jnp.float32),
+            pltpu.VMEM((2, rows + 1, PITCH, LANES), jnp.float32),
         ],
         compiler_params=pltpu.CompilerParams(vmem_limit_bytes=32 << 20),
     )(blocks.reshape(rows // groups, groups, 3, per_owner, LANES), *consts)
@@ -171,9 +188,9 @@
     width = 2 * owners
     uses = ((query, gated), (grad, grad_query)), ((value, grad_key), (key, grad_value))
     stores = []
-    flat = wide.reshape(2, owners * PITCH, LANES)
-    for slot in range(2):
-        wide[slot, :, :per_owner] = sums[:, slot].astype(jnp.float32)
+    flat = wide.reshape(2, (owners + 1) * PITCH, LANES)
+    for slot in range(2):
+        wide[slot, :owners, :per_owner] = sums[:, slot].astype(jnp.float32)
         for group in range(channels // width):
             for j in range(2):
                 i = 2 * group + j
@@ -207,7 +224,7 @@
         out_specs=[pl.BlockSpec(memory_space=pltpu.HBM)] * 4,
         out_shape=[jax.ShapeDtypeStruct((tokens, channels), jnp.bfloat16)] * 4,
         scratch_shapes=[
-            pltpu.VMEM((2, owners, PITCH, LANES), jnp.float32),
+            pltpu.VMEM((2, owners + 1, PITCH, LANES), jnp.float32),
             pltpu.VMEM((4, tokens, channels), jnp.bfloat16),
             pltpu.SemaphoreType.DMA((4 * channels // width,)),
         ],

time: 164 us -> 164 us (level)
  no operation moved by 1% of the time
where the time goes in v5:
time: 164 us
  blocking collectives  150 us (91%)
  Pallas kernels  12.9 us (8%)
    all_to_all x1, blocking collectives, body(): lax.all_to_all(packed, axes, split_axis=0, concat_axis=0, tiled=True)  90.8 us
    all_to_all x1, blocking collectives, body(): sums = lax.all_to_all(mixed, axes, split_axis=0, concat_axis=0, tiled=True)  59.1 us
    pallas_call x1, Pallas kernels, mix(): pl.pallas_call(mix_kernel, out_shape=jax.ShapeDtypeStruct((rows, 2, per_o...  6.89 us

profile of v5, /device:TPU:1, one launch (start us, length us, event | category | flops | bytes accessed | tf_op | source)
XLA Modules:
  0.0 163.6 jit_solution(3410347843225539452)
XLA Ops:
  0.6 3.3 %shard_map.138 = bf16[256,3,16,128]{3,2,1,0:T(8,128)(2,1)S(1)} custom-call(bf16[128,4096]{1,0:T(8,128)(2,1)} %query.3, bf16[128,4096]{1,0:T(8,128)(2,1)} %key.3, bf16[128,4096]{1,0:T(8,128)(2,1)} %value.3, bf16[128,4096]{1,0:T(8,128)(2,1)} %grad.3, bf16[1024,512]{1,0:T(8,128)(2,1)} %filt.1), custom_call_target="tpu_custom_call" | custom-call | tf_op jit(solution)/shard_map/pallas_call | solution.py:84
  3.9 0.0 copy-start.4
  3.9 0.0 copy-start.5
  3.9 0.0 copy-start.6
  3.9 0.0 copy-start.7
  4.0 0.0 copy-start.8
  4.0 0.0 copy-start.9
  4.0 90.8 %all_to_all.10 = bf16[256,3,16,128]{3,2,1,0:T(8,128)(2,1)S(1)} all-to-all(bf16[256,3,16,128]{3,2,1,0:T(8,128)(2,1)S(1)} %shard_map.138), channel_id=1, replica_groups=mesh['dp'=32,'ctx'=8] {'dp','ctx'}, dimensions={0} | all-to-all | bytes 6291456 | tf_op jit(solution)/shard_map/all_to_all | solution.py:240
  94.7 0.0 copy-done.4
  94.7 0.0 copy-done.5
  94.7 0.0 copy-done.6
  94.8 0.0 copy-done.7
  94.8 0.0 copy-done.8
  94.8 0.0 copy-done.9
  94.8 6.9 %shard_map.139 = bf16[256,2,16,128]{3,2,1,0:T(8,128)(2,1)S(1)} custom-call(bf16[32,8,3,16,128]{4,3,2,1,0:T(8,128)(2,1)S(1)} %bitcast.1, bf16[512,256]{1,0:T(8,128)(2,1)S(1)} %copy-done.5, bf16[256,256]{1,0:T(8,128)(2,1)S(1)} %copy-done.9, bf16[256,256]{1,0:T(8,128)(2,1)S(1)} %copy-done.8, bf16[256,512]{1,0:T(8,128)(2,1)S(1)} %copy-done.4, ...), custom_call_target="tpu_custom_call" | custom-call | tf_op jit(solution)/shard_map/pallas_call | solution.py:174
  101.7 0.0 copy-start
  101.7 0.0 copy-start.1
  101.7 0.0 copy-start.2
  101.7 0.0 copy-start.3
  101.7 59.1 %all_to_all.11.sums = bf16[256,2,16,128]{3,2,1,0:T(8,128)(2,1)S(1)} all-to-all(bf16[256,2,16,128]{3,2,1,0:T(8,128)(2,1)S(1)} %shard_map.139), channel_id=1, replica_groups=mesh['dp'=32,'ctx'=8] {'dp','ctx'}, dimensions={0} | all-to-all | bytes 4194304 | tf_op jit(solution)/shard_map/all_to_all | solution.py:242
  160.8 0.0 copy-done
  160.8 0.0 copy-done.1
  160.8 0.0 copy-done.2
  160.8 0.0 copy-done.3
  160.9 2.7 %shard_map.140 = (bf16[128,4096]{1,0:T(8,128)(2,1)}, bf16[128,4096]{1,0:T(8,128)(2,1)}, bf16[128,4096]{1,0:T(8,128)(2,1)}, bf16[128,4096]{1,0:T(8,128)(2,1)}) custom-call(bf16[256,2,16,128]{3,2,1,0:T(8,128)(2,1)S(1)} %all_to_all.11.sums, bf16[128,4096]{1,0:T(8,128)(2,1)S(1)} %copy-done, bf16[128,4096]{1,0:T(8,128)(2,1)S(1)} %copy-done.1, ...), custom_call_target="tpu_custom_call" | custom-call | tf_op jit(solution)/shard_map/pallas_call | solution.py:221
Async XLA Ops:
  3.9 90.8 %copy-start.4 = (bf16[256,512]{1,0:T(8,128)(2,1)S(1)}, bf16[256,512]{1,0:T(8,128)(2,1)}, u32[]{:S(2)}) copy-start(bf16[256,512]{1,0:T(8,128)(2,1)} %constant.15.clone.outer_bwd) | copy-start | bytes 786436
  3.9 90.8 %copy-start.5 = (bf16[512,256]{1,0:T(8,128)(2,1)S(1)}, bf16[512,256]{1,0:T(8,128)(2,1)}, u32[]{:S(2)}) copy-start(bf16[512,256]{1,0:T(8,128)(2,1)} %constant.12.clone.outer_fwd) | copy-start | bytes 786436
  3.9 90.8 %copy-start.6 = (f32[256,128]{1,0:T(8,128)S(1)}, f32[256,128]{1,0:T(8,128)}, u32[]{:S(2)}) copy-start(f32[256,128]{1,0:T(8,128)} %constant.17.clone.sin) | copy-start | bytes 393220
  3.9 90.8 %copy-start.7 = (f32[256,128]{1,0:T(8,128)S(1)}, f32[256,128]{1,0:T(8,128)}, u32[]{:S(2)}) copy-start(f32[256,128]{1,0:T(8,128)} %constant.16.clone.cos) | copy-start | bytes 393220
  4.0 90.8 %copy-start.8 = (bf16[256,256]{1,0:T(8,128)(2,1)S(1)}, bf16[256,256]{1,0:T(8,128)(2,1)}, u32[]{:S(2)}) copy-start(bf16[256,256]{1,0:T(8,128)(2,1)} %constant.14.clone.inner_bwd) | copy-start | bytes 393220
  4.0 90.8 %copy-start.9 = (bf16[256,256]{1,0:T(8,128)(2,1)S(1)}, bf16[256,256]{1,0:T(8,128)(2,1)}, u32[]{:S(2)}) copy-start(bf16[256,256]{1,0:T(8,128)(2,1)} %constant.13.clone.inner_fwd) | copy-start | bytes 393220
  101.7 59.2 %copy-start = (bf16[128,4096]{1,0:T(8,128)(2,1)S(1)}, bf16[128,4096]{1,0:T(8,128)(2,1)}, u32[]{:S(2)}) copy-start(bf16[128,4096]{1,0:T(8,128)(2,1)} %query.3) | copy-start | bytes 3145732
  101.7 59.1 %copy-start.1 = (bf16[128,4096]{1,0:T(8,128)(2,1)S(1)}, bf16[128,4096]{1,0:T(8,128)(2,1)}, u32[]{:S(2)}) copy-start(bf16[128,4096]{1,0:T(8,128)(2,1)} %key.3) | copy-start | bytes 3145732
  101.7 59.1 %copy-start.2 = (bf16[128,4096]{1,0:T(8,128)(2,1)S(1)}, bf16[128,4096]{1,0:T(8,128)(2,1)}, u32[]{:S(2)}) copy-start(bf16[128,4096]{1,0:T(8,128)(2,1)} %value.3) | copy-start | bytes 3145732
  101.7 59.1 %copy-start.3 = (bf16[128,4096]{1,0:T(8,128)(2,1)S(1)}, bf16[128,4096]{1,0:T(8,128)(2,1)}, u32[]{:S(2)}) copy-start(bf16[128,4096]{1,0:T(8,128)(2,1)} %grad.3) | copy-start | bytes 3145732

commit v6 on v5

--- a/solution.py
+++ b/solution.py
@@ -71,10 +71,8 @@
         loads[2 * slot + 1].wait()
         for i in range(per_owner):
             columns = slice(i * owners, (i + 1) * owners)
-            prod = raw[2 * slot, :, columns].astype(jnp.float32) * raw[
-                2 * slot + 1, :, columns
-            ].astype(jnp.float32)
-            spread[slot, pl.ds(i, owners, stride=PITCH), :] = turned(prod.astype(jnp.bfloat16))
+            prod = raw[2 * slot, :, columns] * raw[2 * slot + 1, :, columns]
+            spread[slot, pl.ds(i, owners, stride=PITCH), :] = turned(prod)
         send(slot, 0, owners)
 
 
@@ -195,11 +193,9 @@
             for j in range(2):
                 i = 2 * group + j
                 columns = slice(i * owners, (i + 1) * owners)
-                tokens = flat[slot, pl.ds(i, owners, stride=PITCH), :].T
+                tokens = flat[slot, pl.ds(i, owners, stride=PITCH), :].T.astype(jnp.bfloat16)
                 for k, (source, _) in enumerate(uses[slot]):
-                    ready[2 * slot + k, :, columns] = (
-                        source[:, columns].astype(jnp.float32) * tokens
-                    ).astype(jnp.bfloat16)
+                    ready[2 * slot + k, :, columns] = source[:, columns] * tokens
             columns = pl.ds(group * width, width)
             for k, (_, target) in enumerate(uses[slot]):
                 stores.append(

time: 164 us -> 163 us (level)
  no operation moved by 1% of the time
where the time goes in v6:
time: 163 us
  blocking collectives  150 us (92%)
  Pallas kernels  12.6 us (8%)
    all_to_all x1, blocking collectives, body(): lax.all_to_all(packed, axes, split_axis=0, concat_axis=0, tiled=True)  90.8 us
    all_to_all x1, blocking collectives, body(): sums = lax.all_to_all(mixed, axes, split_axis=0, concat_axis=0, tiled=True)  59.1 us
    pallas_call x1, Pallas kernels, mix(): pl.pallas_call(mix_kernel, out_shape=jax.ShapeDtypeStruct((rows, 2, per_o...  6.89 us

profile of v6, /device:TPU:1, one launch (start us, length us, event | category | flops | bytes accessed | tf_op | source)
XLA Modules:
  0.0 163.3 jit_solution(101918436622969410)
XLA Ops:
  0.6 3.2 %shard_map.138 = bf16[256,3,16,128]{3,2,1,0:T(8,128)(2,1)S(1)} custom-call(bf16[128,4096]{1,0:T(8,128)(2,1)} %query.3, bf16[128,4096]{1,0:T(8,128)(2,1)} %key.3, bf16[128,4096]{1,0:T(8,128)(2,1)} %value.3, bf16[128,4096]{1,0:T(8,128)(2,1)} %grad.3, bf16[1024,512]{1,0:T(8,128)(2,1)} %filt.1), custom_call_target="tpu_custom_call" | custom-call | tf_op jit(solution)/shard_map/pallas_call | solution.py:82
  3.8 0.0 copy-start.4
  3.8 0.0 copy-start.5
  3.9 0.0 copy-start.6
  3.9 0.0 copy-start.7
  3.9 0.0 copy-start.8
  3.9 0.0 copy-start.9
  3.9 90.8 %all_to_all.10 = bf16[256,3,16,128]{3,2,1,0:T(8,128)(2,1)S(1)} all-to-all(bf16[256,3,16,128]{3,2,1,0:T(8,128)(2,1)S(1)} %shard_map.138), channel_id=1, replica_groups=mesh['dp'=32,'ctx'=8] {'dp','ctx'}, dimensions={0} | all-to-all | bytes 6291456 | tf_op jit(solution)/shard_map/all_to_all | solution.py:236
  94.7 0.0 copy-done.4
  94.7 0.0 copy-done.5
  94.7 0.0 copy-done.6
  94.7 0.0 copy-done.7
  94.7 0.0 copy-done.8
  94.7 0.0 copy-done.9
  94.7 6.9 %shard_map.139 = bf16[256,2,16,128]{3,2,1,0:T(8,128)(2,1)S(1)} custom-call(bf16[32,8,3,16,128]{4,3,2,1,0:T(8,128)(2,1)S(1)} %bitcast.1, bf16[512,256]{1,0:T(8,128)(2,1)S(1)} %copy-done.5, bf16[256,256]{1,0:T(8,128)(2,1)S(1)} %copy-done.9, bf16[256,256]{1,0:T(8,128)(2,1)S(1)} %copy-done.8, bf16[256,512]{1,0:T(8,128)(2,1)S(1)} %copy-done.4, ...), custom_call_target="tpu_custom_call" | custom-call | tf_op jit(solution)/shard_map/pallas_call | solution.py:172
  101.6 0.0 copy-start
  101.6 0.0 copy-start.1
  101.6 0.0 copy-start.2
  101.6 0.0 copy-start.3
  101.7 59.1 %all_to_all.11.sums = bf16[256,2,16,128]{3,2,1,0:T(8,128)(2,1)S(1)} all-to-all(bf16[256,2,16,128]{3,2,1,0:T(8,128)(2,1)S(1)} %shard_map.139), channel_id=1, replica_groups=mesh['dp'=32,'ctx'=8] {'dp','ctx'}, dimensions={0} | all-to-all | bytes 4194304 | tf_op jit(solution)/shard_map/all_to_all | solution.py:238
  160.8 0.0 copy-done
  160.8 0.0 copy-done.1
  160.8 0.0 copy-done.2
  160.8 0.0 copy-done.3
  160.8 2.5 %shard_map.140 = (bf16[128,4096]{1,0:T(8,128)(2,1)}, bf16[128,4096]{1,0:T(8,128)(2,1)}, bf16[128,4096]{1,0:T(8,128)(2,1)}, bf16[128,4096]{1,0:T(8,128)(2,1)}) custom-call(bf16[256,2,16,128]{3,2,1,0:T(8,128)(2,1)S(1)} %all_to_all.11.sums, bf16[128,4096]{1,0:T(8,128)(2,1)S(1)} %copy-done, bf16[128,4096]{1,0:T(8,128)(2,1)S(1)} %copy-done.1, ...), custom_call_target="tpu_custom_call" | custom-call | tf_op jit(solution)/shard_map/pallas_call | solution.py:217
Async XLA Ops:
  3.8 90.8 %copy-start.4 = (bf16[256,512]{1,0:T(8,128)(2,1)S(1)}, bf16[256,512]{1,0:T(8,128)(2,1)}, u32[]{:S(2)}) copy-start(bf16[256,512]{1,0:T(8,128)(2,1)} %constant.15.clone.outer_bwd) | copy-start | bytes 786436
  3.8 90.8 %copy-start.5 = (bf16[512,256]{1,0:T(8,128)(2,1)S(1)}, bf16[512,256]{1,0:T(8,128)(2,1)}, u32[]{:S(2)}) copy-start(bf16[512,256]{1,0:T(8,128)(2,1)} %constant.12.clone.outer_fwd) | copy-start | bytes 786436
  3.9 90.8 %copy-start.6 = (f32[256,128]{1,0:T(8,128)S(1)}, f32[256,128]{1,0:T(8,128)}, u32[]{:S(2)}) copy-start(f32[256,128]{1,0:T(8,128)} %constant.17.clone.sin) | copy-start | bytes 393220
  3.9 90.8 %copy-start.7 = (f32[256,128]{1,0:T(8,128)S(1)}, f32[256,128]{1,0:T(8,128)}, u32[]{:S(2)}) copy-start(f32[256,128]{1,0:T(8,128)} %constant.16.clone.cos) | copy-start | bytes 393220
  3.9 90.8 %copy-start.8 = (bf16[256,256]{1,0:T(8,128)(2,1)S(1)}, bf16[256,256]{1,0:T(8,128)(2,1)}, u32[]{:S(2)}) copy-start(bf16[256,256]{1,0:T(8,128)(2,1)} %constant.14.clone.inner_bwd) | copy-start | bytes 393220
  3.9 90.8 %copy-start.9 = (bf16[256,256]{1,0:T(8,128)(2,1)S(1)}, bf16[256,256]{1,0:T(8,128)(2,1)}, u32[]{:S(2)}) copy-start(bf16[256,256]{1,0:T(8,128)(2,1)} %constant.13.clone.inner_fwd) | copy-start | bytes 393220
  101.6 59.2 %copy-start = (bf16[128,4096]{1,0:T(8,128)(2,1)S(1)}, bf16[128,4096]{1,0:T(8,128)(2,1)}, u32[]{:S(2)}) copy-start(bf16[128,4096]{1,0:T(8,128)(2,1)} %query.3) | copy-start | bytes 3145732
  101.6 59.1 %copy-start.1 = (bf16[128,4096]{1,0:T(8,128)(2,1)S(1)}, bf16[128,4096]{1,0:T(8,128)(2,1)}, u32[]{:S(2)}) copy-start(bf16[128,4096]{1,0:T(8,128)(2,1)} %key.3) | copy-start | bytes 3145732
  101.6 59.1 %copy-start.2 = (bf16[128,4096]{1,0:T(8,128)(2,1)S(1)}, bf16[128,4096]{1,0:T(8,128)(2,1)}, u32[]{:S(2)}) copy-start(bf16[128,4096]{1,0:T(8,128)(2,1)} %value.3) | copy-start | bytes 3145732
  101.6 59.1 %copy-start.3 = (bf16[128,4096]{1,0:T(8,128)(2,1)S(1)}, bf16[128,4096]{1,0:T(8,128)(2,1)}, u32[]{:S(2)}) copy-start(bf16[128,4096]{1,0:T(8,128)(2,1)} %grad.3) | copy-start | bytes 3145732
